TPU v7x, 32 devices: a whole 2x2x4 slice. The times are simulated.
32 devices in a mesh: shard: 8 (over z, y), tensor: 4 (over x, core).
Axes of the slice: x: 2, y: 2, z: 4, core: 2. Of those that a mesh axis runs over, the one named last changes fastest.
Arguments:
- inputs: bfloat16 [8192, 768], P(('shard', 'tensor')), may hold values from -6 to 6
- w_query: bfloat16 [768, 768], P('shard', 'tensor'), may hold values from -0.21875 to 0.21875
- w_key: bfloat16 [768, 768], P('shard', 'tensor'), may hold values from -0.21875 to 0.21875
- w_value: bfloat16 [768, 768], P('shard', 'tensor'), may hold values from -0.21875 to 0.21875
- bias_query: float32 [768], replicated, may hold values from -1 to 1
- bias_value: float32 [768], replicated, may hold values from -0.1 to 0.1
- w_out: bfloat16 [768, 768], P('tensor', 'shard'), may hold values from -4 to 4
- bias_out: float32 [768], replicated, may hold values from -1.5 to 1.5
- gain_one: float32 [768], replicated, may hold values from 0.5 to 1.5
- shift_one: float32 [768], replicated, may hold values from -1 to 1
- gain_two: float32 [768], replicated, may hold values from 0.5 to 1.5
- shift_two: float32 [768], replicated, may hold values from -1 to 1
- w_up: bfloat16 [768, 3072], P('shard', 'tensor'), may hold values from -0.21875 to 0.21875
- bias_up: float32 [3072], replicated, may hold values from -1.5 to 1.5
- w_down: bfloat16 [3072, 768], P('tensor', 'shard'), may hold values from -0.109375 to 0.109375
- bias_down: float32 [768], replicated, may hold values from -1.5 to 1.5
- cotangent: bfloat16 [8192, 768], P(('shard', 'tensor')), may hold values from -6 to 6
Outputs:
- output: float32 [8192, 768], P(('shard', 'tensor'))
- grad_inputs: float32 [8192, 768], P(('shard', 'tensor'))
- grad_w_query: float32 [768, 768], P('shard', 'tensor')
- grad_w_key: float32 [768, 768], P('shard', 'tensor')
- grad_w_value: float32 [768, 768], P('shard', 'tensor')
- grad_bias_query: float32 [768], replicated
- grad_bias_value: float32 [768], replicated
- grad_w_out: float32 [768, 768], P('tensor', 'shard')
- grad_bias_out: float32 [768], replicated
- grad_gain_one: float32 [768], replicated
- grad_shift_one: float32 [768], replicated
- grad_gain_two: float32 [768], replicated
- grad_shift_two: float32 [768], replicated
- grad_w_up: float32 [768, 3072], P('shard', 'tensor')
- grad_bias_up: float32 [3072], replicated
- grad_w_down: float32 [3072, 768], P('tensor', 'shard')
- grad_bias_down: float32 [768], replicated
All inputs are finite; a program needn't handle non-finite values.
Results may differ from a plain program's by a relative error of at most 0.02.
Values may be sent and summed in bfloat16 or wider, within the bound.
A program may use at most 128 MiB of HBM per device.

v0:
```python
import math

import jax
import jax.numpy as jnp
from jax import lax
from jax.sharding import PartitionSpec as P

HD = 64


epsilon = 1e-05


def normalize(matrix, gain_vec, shift_vec):
    center = matrix - jnp.mean(matrix, axis=1, keepdims=True)
    inverse = lax.rsqrt(jnp.mean(center * center, axis=1, keepdims=True) + epsilon)
    unit_rows = center * inverse
    return (unit_rows * gain_vec + shift_vec, unit_rows, inverse)


def norm_backward(grad_normed, unit_rows, inverse, gain_vec):
    grad_unit = grad_normed * gain_vec
    first_mean = jnp.mean(grad_unit, axis=1, keepdims=True)
    second_mean = jnp.mean(grad_unit * unit_rows, axis=1, keepdims=True)
    grad_rows = inverse * (grad_unit - first_mean - unit_rows * second_mean)
    return (grad_rows, jnp.sum(grad_normed * unit_rows, axis=0), jnp.sum(grad_normed, axis=0))


def exact_gelu(values):
    return jax.nn.gelu(values, approximate=False)


def attention_forward(queries, key_rows, value_rows, score_scale):
    length, head_count, head_size = queries.shape
    block_rows = min(512, length)
    blocks = queries.reshape(length // block_rows, block_rows, head_count, head_size)

    def one_block(query_block):
        scores = (
            jnp.einsum("qhd,khd->hqk", query_block, key_rows, preferred_element_type=jnp.float32)
            * score_scale
        )
        top_score = jnp.max(scores, axis=2, keepdims=True)
        exponent = jnp.exp(scores - top_score)
        row_total = jnp.sum(exponent, axis=2, keepdims=True)
        soft_low = (exponent / row_total).astype(jnp.bfloat16)
        mixture = jnp.einsum(
            "hqk,khd->qhd", soft_low, value_rows, preferred_element_type=jnp.float32
        )
        return (mixture.astype(jnp.bfloat16), (top_score + jnp.log(row_total))[:, :, 0])

    mixture, log_total = lax.map(one_block, blocks)
    return (mixture.reshape(length, head_count * head_size), log_total)


def attention_backward(queries, key_rows, value_rows, grad_mixture, log_total, score_scale):
    length, head_count, head_size = queries.shape
    block_rows = min(512, length)
    block_count = length // block_rows
    query_blocks = queries.reshape(block_count, block_rows, head_count, head_size)
    grad_blocks = grad_mixture.reshape(block_count, block_rows, head_count, head_size)

    def one_block(carried, pieces):
        grad_keys, grad_values = carried
        query_block, grad_block, log_block = pieces
        scores = (
            jnp.einsum("qhd,khd->hqk", query_block, key_rows, preferred_element_type=jnp.float32)
            * score_scale
        )
        soft_weights = jnp.exp(scores - log_block[:, :, None])
        grad_soft = jnp.einsum(
            "qhd,khd->hqk", grad_block, value_rows, preferred_element_type=jnp.float32
        )
        inner_sum = jnp.sum(grad_soft * soft_weights, axis=2, keepdims=True)
        grad_scores = (soft_weights * (grad_soft - inner_sum) * score_scale).astype(jnp.bfloat16)
        grad_query = jnp.einsum(
            "hqk,khd->qhd", grad_scores, key_rows, preferred_element_type=jnp.float32
        )
        grad_keys = grad_keys + jnp.einsum(
            "hqk,qhd->khd", grad_scores, query_block, preferred_element_type=jnp.float32
        )
        grad_values = grad_values + jnp.einsum(
            "hqk,qhd->khd",
            soft_weights.astype(jnp.bfloat16),
            grad_block,
            preferred_element_type=jnp.float32,
        )
        return ((grad_keys, grad_values), grad_query)

    zero_grads = jnp.zeros(queries.shape, jnp.float32)
    (grad_keys, grad_values), grad_query = lax.scan(
        one_block, (zero_grads, zero_grads), (query_blocks, grad_blocks, log_total)
    )
    return (grad_query.reshape(length, head_count, head_size), grad_keys, grad_values)


def shards(
    inputs,
    w_query,
    w_key,
    w_value,
    bias_query,
    bias_value,
    w_out,
    bias_out,
    gain_one,
    shift_one,
    gain_two,
    shift_two,
    w_up,
    bias_up,
    w_down,
    bias_down,
    cotangent,
):
    full_query, full_key, full_value, full_out, full_up, full_down = (
        lax.all_gather(w_query, "shard", axis=0, tiled=True),
        lax.all_gather(w_key, "shard", axis=0, tiled=True),
        lax.all_gather(w_value, "shard", axis=0, tiled=True),
        lax.all_gather(w_out, "shard", axis=1, tiled=True),
        lax.all_gather(w_up, "shard", axis=0, tiled=True),
        lax.all_gather(w_down, "shard", axis=1, tiled=True),
    )
    head_cols = full_query.shape[1]
    unit_count = full_up.shape[1]
    head_size = HD
    head_count = head_cols // head_size
    tensor_index = lax.axis_index("tensor")
    query_bias = lax.dynamic_slice_in_dim(bias_query, tensor_index * head_cols, head_cols)
    value_bias = lax.dynamic_slice_in_dim(bias_value, tensor_index * head_cols, head_cols)
    up_bias = lax.dynamic_slice_in_dim(bias_up, tensor_index * unit_count, unit_count)
    score_scale = 1.0 / math.sqrt(head_size)
    frames = inputs.astype(jnp.float32)
    normed_one, unit_one, inverse_one = normalize(frames, gain_one, shift_one)
    rows_one = lax.all_gather(normed_one.astype(jnp.bfloat16), "tensor", axis=0, tiled=True)
    length = rows_one.shape[0]
    queries = (
        (jnp.dot(rows_one, full_query, preferred_element_type=jnp.float32) + query_bias)
        .astype(jnp.bfloat16)
        .reshape(length, head_count, head_size)
    )
    key_rows = (
        jnp.dot(rows_one, full_key, preferred_element_type=jnp.float32)
        .astype(jnp.bfloat16)
        .reshape(length, head_count, head_size)
    )
    value_rows = (
        (jnp.dot(rows_one, full_value, preferred_element_type=jnp.float32) + value_bias)
        .astype(jnp.bfloat16)
        .reshape(length, head_count, head_size)
    )
    attended, log_total = attention_forward(queries, key_rows, value_rows, score_scale)
    partial_one = jnp.dot(attended, full_out, preferred_element_type=jnp.float32)
    branch_one = lax.psum_scatter(
        partial_one.astype(jnp.bfloat16), "tensor", scatter_dimension=0, tiled=True
    ).astype(jnp.float32)
    hidden_state = frames + branch_one + bias_out
    normed_two, unit_two, inverse_two = normalize(hidden_state, gain_two, shift_two)
    rows_two = lax.all_gather(normed_two.astype(jnp.bfloat16), "tensor", axis=0, tiled=True)
    pre_act = jnp.dot(rows_two, full_up, preferred_element_type=jnp.float32) + up_bias
    activated = exact_gelu(pre_act).astype(jnp.bfloat16)
    partial_two = jnp.dot(activated, full_down, preferred_element_type=jnp.float32)
    branch_two = lax.psum_scatter(
        partial_two.astype(jnp.bfloat16), "tensor", scatter_dimension=0, tiled=True
    ).astype(jnp.float32)
    output = hidden_state + branch_two + bias_down
    back_query, back_key, back_value, back_out, back_up, back_down = (
        full_query,
        full_key,
        full_value,
        full_out,
        full_up,
        full_down,
    )
    grad_output = cotangent.astype(jnp.float32)
    grad_rows_out = lax.all_gather(cotangent, "tensor", axis=0, tiled=True)
    grad_w_down = jnp.einsum(
        "tf,td->fd", activated, grad_rows_out, preferred_element_type=jnp.float32
    )
    grad_bias_down = jnp.sum(grad_output, axis=0)
    grad_act = jnp.einsum("td,fd->tf", grad_rows_out, back_down, preferred_element_type=jnp.float32)
    _, gelu_pull = jax.vjp(exact_gelu, pre_act)
    grad_pre = gelu_pull(grad_act)[0]
    grad_up_bias = jnp.sum(grad_pre, axis=0)
    grad_pre_low = grad_pre.astype(jnp.bfloat16)
    grad_w_up = jnp.einsum("td,tf->df", rows_two, grad_pre_low, preferred_element_type=jnp.float32)
    back_two = jnp.einsum("tf,df->td", grad_pre_low, back_up, preferred_element_type=jnp.float32)
    grad_normed_two = lax.psum_scatter(
        back_two.astype(jnp.bfloat16), "tensor", scatter_dimension=0, tiled=True
    ).astype(jnp.float32)
    grad_rows_two, grad_gain_two, grad_shift_two = norm_backward(
        grad_normed_two, unit_two, inverse_two, gain_two
    )
    grad_hidden = grad_output + grad_rows_two
    grad_rows_hidden = lax.all_gather(
        grad_hidden.astype(jnp.bfloat16), "tensor", axis=0, tiled=True
    )
    grad_w_out = jnp.einsum(
        "tc,td->cd", attended, grad_rows_hidden, preferred_element_type=jnp.float32
    )
    grad_bias_out = jnp.sum(grad_hidden, axis=0)
    grad_attended = (
        jnp.einsum("td,cd->tc", grad_rows_hidden, back_out, preferred_element_type=jnp.float32)
        .astype(jnp.bfloat16)
        .reshape(length, head_count, head_size)
    )
    grad_queries, grad_keys, grad_values = attention_backward(
        queries, key_rows, value_rows, grad_attended, log_total, score_scale
    )
    grad_query_bias = jnp.sum(grad_queries, axis=0).reshape(head_cols)
    grad_value_bias = jnp.sum(grad_values, axis=0).reshape(head_cols)
    low_queries = grad_queries.astype(jnp.bfloat16).reshape(length, head_cols)
    low_keys = grad_keys.astype(jnp.bfloat16).reshape(length, head_cols)
    low_values = grad_values.astype(jnp.bfloat16).reshape(length, head_cols)
    grad_w_query = jnp.einsum(
        "td,tc->dc", rows_one, low_queries, preferred_element_type=jnp.float32
    )
    grad_w_key = jnp.einsum("td,tc->dc", rows_one, low_keys, preferred_element_type=jnp.float32)
    grad_w_value = jnp.einsum("td,tc->dc", rows_one, low_values, preferred_element_type=jnp.float32)
    back_one = (
        jnp.einsum("tc,dc->td", low_queries, back_query, preferred_element_type=jnp.float32)
        + jnp.einsum("tc,dc->td", low_keys, back_key, preferred_element_type=jnp.float32)
        + jnp.einsum("tc,dc->td", low_values, back_value, preferred_element_type=jnp.float32)
    )
    grad_normed_one = lax.psum_scatter(
        back_one.astype(jnp.bfloat16), "tensor", scatter_dimension=0, tiled=True
    ).astype(jnp.float32)
    grad_rows_one, grad_gain_one, grad_shift_one = norm_backward(
        grad_normed_one, unit_one, inverse_one, gain_one
    )
    grad_inputs = grad_hidden + grad_rows_one
    summed_query, summed_key, summed_value, summed_out, summed_up, summed_down = (
        lax.psum_scatter(grad_w_query, "shard", scatter_dimension=0, tiled=True),
        lax.psum_scatter(grad_w_key, "shard", scatter_dimension=0, tiled=True),
        lax.psum_scatter(grad_w_value, "shard", scatter_dimension=0, tiled=True),
        lax.psum_scatter(grad_w_out, "shard", scatter_dimension=1, tiled=True),
        lax.psum_scatter(grad_w_up, "shard", scatter_dimension=0, tiled=True),
        lax.psum_scatter(grad_w_down, "shard", scatter_dimension=1, tiled=True),
    )
    width = gain_one.shape[0]
    full_query_bias = lax.dynamic_update_slice_in_dim(
        jnp.zeros((width,), jnp.float32), grad_query_bias, tensor_index * head_cols, 0
    )
    full_value_bias = lax.dynamic_update_slice_in_dim(
        jnp.zeros((width,), jnp.float32), grad_value_bias, tensor_index * head_cols, 0
    )
    full_up_bias = lax.dynamic_update_slice_in_dim(
        jnp.zeros(bias_up.shape, jnp.float32), grad_up_bias, tensor_index * unit_count, 0
    )
    small_sums = lax.psum(
        (
            full_query_bias,
            full_value_bias,
            grad_bias_out,
            grad_gain_one,
            grad_shift_one,
            grad_gain_two,
            grad_shift_two,
            full_up_bias,
            grad_bias_down,
        ),
        ("shard", "tensor"),
    )
    return (
        output,
        grad_inputs,
        summed_query,
        summed_key,
        summed_value,
        small_sums[0],
        small_sums[1],
        summed_out,
        small_sums[2],
        small_sums[3],
        small_sums[4],
        small_sums[5],
        small_sums[6],
        summed_up,
        small_sums[7],
        summed_down,
        small_sums[8],
    )


def solution(mesh):
    placed = (
        P(("shard", "tensor"), None),
        P("shard", "tensor"),
        P("shard", "tensor"),
        P("shard", "tensor"),
        P(),
        P(),
        P("tensor", "shard"),
        P(),
        P(),
        P(),
        P(),
        P(),
        P("shard", "tensor"),
        P(),
        P("tensor", "shard"),
        P(),
        P(("shard", "tensor"), None),
    )
    return jax.shard_map(
        shards,
        mesh=mesh,
        in_specs=placed,
        out_specs=(
            P(("shard", "tensor"), None),
            P(("shard", "tensor"), None),
            P("shard", "tensor"),
            P("shard", "tensor"),
            P("shard", "tensor"),
            P(),
            P(),
            P("tensor", "shard"),
            P(),
            P(),
            P(),
            P(),
            P(),
            P("shard", "tensor"),
            P(),
            P("tensor", "shard"),
            P(),
        ),
        check_vma=False,
    )
```

profile of v0, /device:TPU:0, one launch (start us, length us, event | category | flops | bytes accessed | tf_op | source)
XLA Modules:
  0.0 913.6 jit_solution(16389283673463059674)
XLA Ops:
  15.0 32.9 %all_gather.34 = bf16[192,768]{0,1:T(8,128)(2,1)S(1)} all-gather(bf16[192,96]{0,1:T(8,128)(2,1)S(1)} %copy.44), channel_id=1, replica_groups=mesh['shard'=8,'tensor'=4] {'shard'}, dimensions={1}, use_global_device_ids=true | all-gather | bytes 331776 | tf_op jit(solution)/shard_map/all_gather | solution.py:120
  48.0 31.4 %all_gather.31 = bf16[768,192]{1,0:T(8,128)(2,1)S(1)} all-gather(bf16[96,192]{1,0:T(8,128)(2,1)} %param.22), channel_id=1, replica_groups=mesh['shard'=8,'tensor'=4] {'shard'}, dimensions={0}, use_global_device_ids=true | all-gather | bytes 331776 | tf_op jit(solution)/shard_map/all_gather | solution.py:117
  79.4 31.4 %all_gather.32 = bf16[768,192]{1,0:T(8,128)(2,1)S(1)} all-gather(bf16[96,192]{1,0:T(8,128)(2,1)} %param.23), channel_id=1, replica_groups=mesh['shard'=8,'tensor'=4] {'shard'}, dimensions={0}, use_global_device_ids=true | all-gather | bytes 331776 | tf_op jit(solution)/shard_map/all_gather | solution.py:118
  110.8 31.0 %all_gather.33 = bf16[768,192]{1,0:T(8,128)(2,1)S(1)} all-gather(bf16[96,192]{1,0:T(8,128)(2,1)S(1)} %copy-done.22), channel_id=1, replica_groups=mesh['shard'=8,'tensor'=4] {'shard'}, dimensions={0}, use_global_device_ids=true | all-gather | bytes 331776 | tf_op jit(solution)/shard_map/all_gather | solution.py:119
  161.6 28.4 %reduce-scatter.13.cloned.1.call-done = bf16[256,768]{1,0:T(8,128)(2,1)} async-done(((bf16[1024,768]{1,0:T(8,128)(2,1)}), bf16[256,768]{1,0:T(8,128)(2,1)}) %reduce-scatter.13.cloned.1.call-update) | async-done | bytes 393232 | tf_op jit(solution)/shard_map/reduce_scatter | solution.py:154
  206.2 20.1 %all-gather.9.cloned.1.call-done = bf16[1024,768]{1,0:T(8,128)(2,1)} async-done(((bf16[256,768]{1,0:T(8,128)(2,1)}), bf16[1024,768]{1,0:T(8,128)(2,1)}) %all-gather.9.cloned.1.call-update) | async-done | bytes 1572880 | tf_op jit(solution)/shard_map/all_gather | solution.py:159
  231.0 39.1 %all-gather.13.cloned.1.call-done = bf16[768,768]{0,1:T(8,128)(2,1)} async-done(((bf16[768,96]{0,1:T(8,128)(2,1)}), bf16[768,768]{0,1:T(8,128)(2,1)}) %all-gather.13.cloned.1.call-update) | async-done | bytes 1179664 | tf_op jit(solution)/shard_map/all_gather | solution.py:122
  270.1 19.7 %all-gather.15.cloned.1.call-done = bf16[1024,768]{1,0:T(8,128)(2,1)} async-done(((bf16[256,768]{1,0:T(8,128)(2,1)}), bf16[1024,768]{1,0:T(8,128)(2,1)}) %all-gather.15.cloned.1.call-update) | async-done | bytes 1572880 | tf_op jit(solution)/shard_map/all_gather | solution.py:176
  313.0 21.0 %reduce-scatter.17.cloned.1.call-done = bf16[256,768]{1,0:T(8,128)(2,1)} async-done(((bf16[1024,768]{1,0:T(8,128)(2,1)}), bf16[256,768]{1,0:T(8,128)(2,1)}) %reduce-scatter.17.cloned.1.call-update) | async-done | bytes 393232 | tf_op jit(solution)/shard_map/reduce_scatter | solution.py:188
  336.7 27.9 %reduce-scatter.15.cloned.1.call-done = bf16[256,768]{1,0:T(8,128)(2,1)} async-done(((bf16[1024,768]{1,0:T(8,128)(2,1)}), bf16[256,768]{1,0:T(8,128)(2,1)}) %reduce-scatter.15.cloned.1.call-update) | async-done | bytes 393232 | tf_op jit(solution)/shard_map/reduce_scatter | solution.py:163
  368.8 19.3 %all-gather.17.cloned.1.call-done = bf16[1024,768]{1,0:T(8,128)(2,1)} async-done(((bf16[256,768]{1,0:T(8,128)(2,1)}), bf16[1024,768]{1,0:T(8,128)(2,1)}) %all-gather.17.cloned.1.call-update) | async-done | bytes 1572880 | tf_op jit(solution)/shard_map/all_gather | solution.py:195
  394.1 71.2 %while.28 = (s32[]{:T(128)}, f32[1024,3,64]{0,2,1:T(8,128)}, f32[1024,3,64]{0,2,1:T(8,128)S(1)}, f32[2,512,3,64]{1,3,2,0:T(8,128)}, bf16[2,512,3,64]{1,3,2,0:T(8...) while((s32[]{:T(128)}, f32[1024,3,64]{0,2,1:T(8,128)}, ...), condition=%wide.region_15.16_spmd.clone, body=%wide.region_13.15_spmd.clone.sunk | while | flops 1040454656 | bytes 99930288 | solution.py:91
  402.2 14.2 %fusion.195 = f32[1024,3,64]{0,2,1:T(8,128)} fusion(f32[3,512,1024]{2,1,0:T(8,128)} %fusion.193, f32[3,512,1024]{2,1,0:T(8,128)} %copy-done, f32[3,512]{1,0:T(4,128)S(1)} %dynamic-slice_bitcast_fusion.2, f32[1024,3,64]{0,2,1:T(8,128)} %get-tuple-element.373, pred[]{:T(512)S(6)} %compare.3, bf16[2,512,3,64]{1,3,2,0:T(8,128)(2,1)S(1)} %get-tuple-element.387, ...), kind=kOutput, calls=%fused_computation.32.clone.1 | convolution fusion | flops 215878144 | bytes 26951684 | tf_op jit(solution)/shard_map/while/body/eval_jaxpr/hqk,qhd->khd/dot_general | solution.py:79
  416.3 13.3 %fusion.197 = f32[2,512,3,64]{1,3,2,0:T(8,128)} fusion(f32[2,512,3,64]{1,3,2,0:T(8,128)} %get-tuple-element.375, s32[]{:T(128)S(6)} %copy.68, bf16[1024,3,64]{0,2,1:T(8,128)(2,1)S(1)} %get-tuple-element.388, f32[3,512,1024]{2,1,0:T(8,128)} %fusion.193, f32[3,512,1024]{2,1,0:T(8,128)} %copy-done, f32[3,512]{1,0:T(4,128)S(1)} %dynamic-slice_bitcast_fusion.2), kind=kOutput, calls=%fused_computation.34.clone.1 | convolution fusion | flops 215484928 | bytes 25968644 | tf_op jit(solution)/shard_map/while/body/eval_jaxpr/hqk,khd->qhd/dot_general | solution.py:76
  437.7 14.4 %fusion.195 = f32[1024,3,64]{0,2,1:T(8,128)} fusion(f32[3,512,1024]{2,1,0:T(8,128)} %fusion.193, f32[3,512,1024]{2,1,0:T(8,128)} %copy-done, f32[3,512]{1,0:T(4,128)S(1)} %dynamic-slice_bitcast_fusion.2, f32[1024,3,64]{0,2,1:T(8,128)} %get-tuple-element.373, pred[]{:T(512)S(6)} %compare.3, bf16[2,512,3,64]{1,3,2,0:T(8,128)(2,1)S(1)} %get-tuple-element.387, ...), kind=kOutput, calls=%fused_computation.32.clone.1 | convolution fusion | flops 215878144 | bytes 26951684 | tf_op jit(solution)/shard_map/while/body/eval_jaxpr/hqk,qhd->khd/dot_general | solution.py:79
  452.1 13.2 %fusion.197 = f32[2,512,3,64]{1,3,2,0:T(8,128)} fusion(f32[2,512,3,64]{1,3,2,0:T(8,128)} %get-tuple-element.375, s32[]{:T(128)S(6)} %copy.68, bf16[1024,3,64]{0,2,1:T(8,128)(2,1)S(1)} %get-tuple-element.388, f32[3,512,1024]{2,1,0:T(8,128)} %fusion.193, f32[3,512,1024]{2,1,0:T(8,128)} %copy-done, f32[3,512]{1,0:T(4,128)S(1)} %dynamic-slice_bitcast_fusion.2), kind=kOutput, calls=%fused_computation.34.clone.1 | convolution fusion | flops 215484928 | bytes 25968644 | tf_op jit(solution)/shard_map/while/body/eval_jaxpr/hqk,khd->qhd/dot_general | solution.py:76
  492.3 40.4 %reduce-scatter.31.cloned.1.call-done = f32[96,192]{1,0:T(8,128)} async-done(((f32[768,192]{1,0:T(8,128)}), f32[96,192]{1,0:T(8,128)}) %reduce-scatter.31.cloned.1.call-update) | async-done | bytes 73744
  534.4 27.9 %reduce-scatter.19.cloned.1.call-done = bf16[256,768]{1,0:T(8,128)(2,1)} async-done(((bf16[1024,768]{1,0:T(8,128)(2,1)}), bf16[256,768]{1,0:T(8,128)(2,1)}) %reduce-scatter.19.cloned.1.call-update) | async-done | bytes 393232 | tf_op jit(solution)/shard_map/reduce_scatter | solution.py:225
  563.8 42.5 %all-reduce = (f32[768]{0:T(1024)}, f32[768]{0:T(1024)}, f32[768]{0:T(1024)}, f32[768]{0:T(1024)}, f32[768]{0:T(1024)}, /*index=5*/f32[768]{0:T(1024)}, f32[768]{0:T(1024)}, f32[3072]{0:T(1024)}, f32[768]{0:T(1024)}) all-reduce(f32[768]{0:T(1024)S(1)} %dynamic_update_slice.21, ...), channel_id=1, replica_groups=mesh['shard'=8,'tensor'=4] {'shard','tensor'}, use_global_device_ids=true, to_apply=%region_23.24 | all-reduce | flops 9216 | bytes 73728 | tf_op jit(solution)/shard_map/psum | solution.py:250
  608.5 28.1 %reduce-scatter.29.cloned.1.call-done = f32[768,96]{0,1:T(8,128)} async-done(((f32[768,768]{0,1:T(8,128)}), f32[768,96]{0,1:T(8,128)}) %reduce-scatter.29.cloned.1.call-update) | async-done | bytes 294928 | tf_op jit(solution)/shard_map/reduce_scatter | solution.py:238
  636.6 72.4 %reduce-scatter.27.cloned.1.call-done = f32[96,768]{1,0:T(8,128)} async-done(((f32[768,768]{1,0:T(8,128)}), f32[96,768]{1,0:T(8,128)}) %reduce-scatter.27.cloned.1.call-update) | async-done | bytes 294928 | tf_op jit(solution)/shard_map/reduce_scatter | solution.py:237
  709.0 65.9 %reduce-scatter.25.cloned.1.call-done = f32[96,192]{1,0:T(8,128)} async-done(((f32[768,192]{1,0:T(8,128)}), f32[96,192]{1,0:T(8,128)}) %reduce-scatter.25.cloned.1.call-update) | async-done | bytes 73744 | tf_op jit(solution)/shard_map/reduce_scatter | solution.py:235
  774.9 65.4 %reduce-scatter.21.cloned.1.call-done = f32[96,192]{1,0:T(8,128)} async-done(((f32[768,192]{1,0:T(8,128)}), f32[96,192]{1,0:T(8,128)}) %reduce-scatter.21.cloned.1.call-update) | async-done | bytes 73744 | tf_op jit(solution)/shard_map/reduce_scatter | solution.py:233
  840.3 65.8 %reduce-scatter.23.cloned.1.call-done = f32[96,192]{1,0:T(8,128)} async-done(((f32[768,192]{1,0:T(8,128)}), f32[96,192]{1,0:T(8,128)}) %reduce-scatter.23.cloned.1.call-update) | async-done | bytes 73744 | tf_op jit(solution)/shard_map/reduce_scatter | solution.py:234
  (197 shorter events, 141.5 us)
Async XLA Ops:
  8.0 102.8 %copy-start.22 = (bf16[96,192]{1,0:T(8,128)(2,1)S(1)}, bf16[96,192]{1,0:T(8,128)(2,1)}, u32[]{:S(2)}) copy-start(bf16[96,192]{1,0:T(8,128)(2,1)} %param.24) | copy-start | bytes 110596
  8.0 133.8 %all-gather.7.cloned.1.call-start = ((), (), s32[]{:S(2)}) async-start(), calls=%async_computation.10 | async-start | bytes 1966080 | tf_op jit(solution)/shard_map/all_gather | solution.py:135
  12.5 177.5 %reduce-scatter.13.cloned.1.call-start = ((), (), s32[]{:S(2)}) async-start(), calls=%async_computation.11 | async-start | bytes 1966080 | tf_op jit(solution)/shard_map/reduce_scatter | solution.py:154
  48.0 111.2 %copy-start.7 = (bf16[192,768]{0,1:T(8,128)(2,1)}, bf16[192,768]{0,1:T(8,128)(2,1)S(1)}, u32[]{:S(2)}) copy-start(bf16[192,768]{0,1:T(8,128)(2,1)S(1)} %all_gather.34) | copy-start | bytes 884740
  161.0 45.2 %all-gather.11.cloned.1.call-start = ((), (), s32[]{:S(2)}) async-start(), calls=%async_computation.13 | async-start | bytes 1327104 | tf_op jit(solution)/shard_map/all_gather | solution.py:121
  161.6 64.7 %all-gather.9.cloned.1.call-start = ((), (), s32[]{:S(2)}) async-start(), calls=%async_computation.12 | async-start | bytes 1966080 | tf_op jit(solution)/shard_map/all_gather | solution.py:159
  194.6 75.5 %all-gather.13.cloned.1.call-start = ((), (), s32[]{:S(2)}) async-start(), calls=%async_computation.14 | async-start | bytes 1327104 | tf_op jit(solution)/shard_map/all_gather | solution.py:122
  195.1 94.6 %all-gather.15.cloned.1.call-start = ((), (), s32[]{:S(2)}) async-start(), calls=%async_computation.16 | async-start | bytes 1966080 | tf_op jit(solution)/shard_map/all_gather | solution.py:176
  195.9 138.1 %reduce-scatter.17.cloned.1.call-start = ((), (), s32[]{:S(2)}) async-start(), calls=%async_computation.17 | async-start | bytes 1966080 | tf_op jit(solution)/shard_map/reduce_scatter | solution.py:188
  305.6 58.9 %reduce-scatter.15.cloned.1.call-start = ((), (), s32[]{:S(2)}) async-start(), calls=%async_computation.15 | async-start | bytes 1966080 | tf_op jit(solution)/shard_map/reduce_scatter | solution.py:163
  312.9 75.3 %copy-start.8 = (bf16[192,768]{0,1:T(8,128)(2,1)S(1)}, bf16[192,768]{0,1:T(8,128)(2,1)}, u32[]{:S(2)}) copy-start(bf16[192,768]{0,1:T(8,128)(2,1)} %copy-done.7) | copy-start | bytes 884740
  312.9 75.3 %all-gather.17.cloned.1.call-start = ((), (), s32[]{:S(2)}) async-start(), calls=%async_computation.18 | async-start | bytes 1966080 | tf_op jit(solution)/shard_map/all_gather | solution.py:195
  368.6 164.2 %reduce-scatter.31.cloned.1.call-start = ((), (), s32[]{:S(2)}) async-start(), calls=%async_computation.25 | async-start | bytes 884736
  470.0 92.3 %reduce-scatter.19.cloned.1.call-start = ((), (), s32[]{:S(2)}) async-start(), calls=%async_computation.19 | async-start | bytes 1966080 | tf_op jit(solution)/shard_map/reduce_scatter | solution.py:225
  475.7 160.9 %reduce-scatter.29.cloned.1.call-start = ((), (), s32[]{:S(2)}) async-start(), calls=%async_computation.24 | async-start | bytes 2654208 | tf_op jit(solution)/shard_map/reduce_scatter | solution.py:238
  480.3 228.7 %reduce-scatter.27.cloned.1.call-start = ((), (), s32[]{:S(2)}) async-start(), calls=%async_computation.23 | async-start | bytes 2654208 | tf_op jit(solution)/shard_map/reduce_scatter | solution.py:237
  485.2 289.7 %reduce-scatter.25.cloned.1.call-start = ((), (), s32[]{:S(2)}) async-start(), calls=%async_computation.22 | async-start | bytes 884736 | tf_op jit(solution)/shard_map/reduce_scatter | solution.py:235
  486.9 75.4 %copy-start.24 = (f32[768]{0:T(1024)S(1)}, f32[768]{0:T(1024)}, u32[]{:S(2)}) copy-start(f32[768]{0:T(1024)} %param.29) | copy-start | bytes 9220
  486.9 75.4 %copy-start.26 = (f32[256]{0:T(256)S(1)}, f32[256]{0:T(256)}, u32[]{:S(2)}) copy-start(f32[256]{0:T(256)} %copy-done.25) | copy-start | bytes 3076
  486.9 75.4 %copy-start.28 = (f32[256]{0:T(256)S(1)}, f32[256]{0:T(256)}, u32[]{:S(2)}) copy-start(f32[256]{0:T(256)} %copy-done.27) | copy-start | bytes 3076
  486.9 353.3 %reduce-scatter.21.cloned.1.call-start = ((), (), s32[]{:S(2)}) async-start(), calls=%async_computation.20 | async-start | bytes 884736 | tf_op jit(solution)/shard_map/reduce_scatter | solution.py:233
  488.5 75.3 %copy-start.31 = (f32[768]{0:T(1024)S(1)}, f32[768]{0:T(1024)}, u32[]{:S(2)}) copy-start(f32[768]{0:T(1024)} %get-tuple-element.229) | copy-start | bytes 9220
  488.5 75.3 %copy-start.32 = (f32[768]{0:T(1024)S(1)}, f32[768]{0:T(1024)}, u32[]{:S(2)}) copy-start(f32[768]{0:T(1024)} %get-tuple-element.238) | copy-start | bytes 9220
  488.5 417.6 %reduce-scatter.23.cloned.1.call-start = ((), (), s32[]{:S(2)}) async-start(), calls=%async_computation.21 | async-start | bytes 884736 | tf_op jit(solution)/shard_map/reduce_scatter | solution.py:234
  (32 other events, 620.6 us)
Sparse Core Ops, SparseCore 0:
  12.6 22.3 all-gather.6
  161.1 28.8 reduce-scatter.12
  305.8 28.1 reduce-scatter.16
  336.4 28.1 reduce-scatter.14
Sparse Core Ops, SparseCore 1:
  163.9 42.2 all-gather.10
  208.3 17.9 all-gather.8
  228.5 41.5 all-gather.12
  271.7 18.0 all-gather.14
  368.6 19.5 all-gather.16
  470.1 62.6 reduce-scatter.30
  535.1 27.1 reduce-scatter.18
  566.6 69.9 reduce-scatter.28
  640.9 68.0 reduce-scatter.26
  713.2 61.6 reduce-scatter.24
  778.6 61.6 reduce-scatter.20
  844.5 61.5 reduce-scatter.22
where the time goes:
time: 921 us; the launch traced here: 914 us
  waiting for transfers between devices  553 us (60%)
  blocking collectives  169 us (18%)
  matrix products  124 us (13%)
  other arithmetic  29.9 us (3%)
  local copies, waits for them, and re-layouts  19.8 us (2%)
  between operations  16.3 us (2%)
    reduce_scatter x1, waiting for transfers between devices, shards(): lax.psum_scatter(grad_w_up, 'shard', scatter_dimension=0, tiled=True)  72.4 us
    reduce_scatter x1, waiting for transfers between devices, shards(): lax.psum_scatter(grad_w_value, 'shard', scatter_dimension=0, tiled=True)  65.9 us
    reduce_scatter x1, waiting for transfers between devices, shards(): lax.psum_scatter(grad_w_key, 'shard', scatter_dimension=0, tiled=True)  65.8 us
    reduce_scatter x1, waiting for transfers between devices, shards(): lax.psum_scatter(grad_w_query, 'shard', scatter_dimension=0, tiled=True)  65.4 us
    psum x1, blocking collectives, shards(): lax.psum((full_query_bias, full_value_bias, grad_bias_out, grad_gain_one,...  42.5 us
    unnamed x17, waiting for transfers between devices  42.3 us
    all_gather x1, waiting for transfers between devices, shards(): lax.all_gather(w_down, 'shard', axis=1, tiled=True)  39.1 us
    all_gather x1, blocking collectives, shards(): lax.all_gather(w_out, 'shard', axis=1, tiled=True)  32.9 us
  transfers between devices with their start and end apart: 16, of which 15 were waited for; matrix products, arithmetic and copies ran while one was open for 5% of the time, Pallas kernels for 0%

commit v1 on v0

v1 whole, which is shorter than its diff:
```python
import functools
import math

import jax
import jax.numpy as jnp
from jax import lax
from jax.experimental import pallas as pl
from jax.experimental.pallas import tpu as pltpu
from jax.sharding import PartitionSpec as P

HD = 64
MESH = pl.DeviceIdType.MESH
F32 = jnp.float32
BF16 = jnp.bfloat16

epsilon = 1e-05


def normalize(matrix, gain_vec, shift_vec):
    center = matrix - jnp.mean(matrix, axis=1, keepdims=True)
    inverse = lax.rsqrt(jnp.mean(center * center, axis=1, keepdims=True) + epsilon)
    unit_rows = center * inverse
    return (unit_rows * gain_vec + shift_vec, unit_rows, inverse)


def norm_backward(grad_normed, unit_rows, inverse, gain_vec):
    grad_unit = grad_normed * gain_vec
    first_mean = jnp.mean(grad_unit, axis=1, keepdims=True)
    second_mean = jnp.mean(grad_unit * unit_rows, axis=1, keepdims=True)
    grad_rows = inverse * (grad_unit - first_mean - unit_rows * second_mean)
    return (grad_rows, jnp.sum(grad_normed * unit_rows, axis=0), jnp.sum(grad_normed, axis=0))


def exact_gelu(values):
    return jax.nn.gelu(values, approximate=False)


def flip(index, bit):
    return index + bit - 2 * bit * lax.rem(lax.div(index, bit), 2)


def greet(tensor_peers, shard_peers):
    barrier = pltpu.get_barrier_semaphore()
    for peer in tensor_peers:
        pl.semaphore_signal(barrier, inc=1, device_id={"tensor": peer}, device_id_type=MESH)
    for peer in shard_peers:
        pl.semaphore_signal(barrier, inc=1, device_id={"shard": peer}, device_id_type=MESH)
    pl.semaphore_wait(barrier, len(tensor_peers) + len(shard_peers))


def shard_peers_of(me, count):
    return [flip(me, 1)] + [lax.rem(me + 2 * step, count) for step in range(1, count // 2)]


class Tally:
    def __init__(self, send, recv):
        self.send, self.recv, self.used, self.sent = send, recv, 0, []

    def copy(self, source, target, **peer):
        slot = self.used
        self.used += 1
        made = pltpu.make_async_remote_copy(
            src_ref=source,
            dst_ref=target,
            send_sem=self.send.at[slot],
            recv_sem=self.recv.at[slot],
            device_id=peer,
            device_id_type=MESH,
        )
        made.start()
        self.sent.append(made)
        return made

    def finish(self):
        for made in self.sent:
            made.wait_send()


def halves(rows, parts=2):
    size = rows // parts
    return [pl.ds(part * size, size) for part in range(parts)]


def tensor_gather_start(tally, blocks, tensor):
    rows = blocks.shape[1]
    far = [
        tally.copy(blocks.at[tensor, cut], blocks.at[tensor, cut], tensor=flip(tensor, 2))
        for cut in halves(rows)
    ]
    near = [tally.copy(blocks.at[tensor], blocks.at[tensor], tensor=flip(tensor, 1))]
    return far, near


def tensor_gather_end(tally, blocks, tensor, state):
    far, near = state
    rows = blocks.shape[1]
    other = flip(tensor, 2)
    for arrived, cut in zip(far, halves(rows)):
        arrived.wait_recv()
        near.append(
            tally.copy(blocks.at[other, cut], blocks.at[other, cut], tensor=flip(tensor, 1))
        )
    for arrived in near:
        arrived.wait_recv()


def tensor_sum_start(tally, parts, landed, tensor):
    sibling, far = flip(tensor, 1), flip(tensor, 2)
    rows = parts.shape[1]
    passing = [
        tally.copy(parts.at[flip(sibling, 2), cut], landed.at[1, cut], tensor=sibling)
        for cut in halves(rows)
    ]
    own = tally.copy(parts.at[sibling], landed.at[0], tensor=sibling)
    return passing, own


def tensor_sum_pass(tally, parts, landed, mixed, tensor, state):
    far = flip(tensor, 2)
    rows = parts.shape[1]
    across = []
    for arrived, cut in zip(state[0], halves(rows)):
        arrived.wait_recv()
        mixed[cut, :] = (parts[far, cut, :].astype(F32) + landed[1, cut, :].astype(F32)).astype(
            BF16
        )
        across.append(tally.copy(mixed.at[cut], landed.at[2, cut], tensor=far))
    return across


def tensor_sum_end(parts, landed, tensor, state, across):
    state[1].wait_recv()
    for arrived in across:
        arrived.wait_recv()
    return parts[tensor].astype(F32) + landed[0].astype(F32) + landed[2].astype(F32)


def gather_kernel(count, *refs):
    (x_ref, gain_ref, shift_ref, cot_ref, w_refs, rows_ref, cots_ref, full_refs, send, recv,
     local) = (refs[0], refs[1], refs[2], refs[3], refs[4:7], refs[7], refs[8], refs[9:12],
               refs[12], refs[13], refs[14])
    tensor, shard = lax.axis_index("tensor"), lax.axis_index("shard")
    partner = flip(shard, 1)
    peers = shard_peers_of(shard, count)
    greet([flip(tensor, 1), flip(tensor, 2)], peers)
    tally = Tally(send, recv)
    keeps = []
    for place, (w_ref, full) in enumerate(zip(w_refs, full_refs)):
        keep = pltpu.make_async_copy(w_ref, full.at[shard], local.at[place])
        keep.start()
        keeps.append(keep)
    keep = pltpu.make_async_copy(cot_ref, cots_ref.at[tensor], local.at[3])
    keep.start()
    keeps.append(keep)
    straight, beside = [], []

    def send_own(place):
        w_ref, full = w_refs[place], full_refs[place]
        straight.append([
            tally.copy(w_ref, full.at[shard], shard=peer) for peer in peers[1:]
        ])
        beside.append(tally.copy(w_ref, full.at[shard], shard=partner))

    send_own(0)
    rows_ref[tensor] = normalize(x_ref[...].astype(F32), gain_ref[...], shift_ref[...])[0].astype(
        BF16
    )
    rows_state = tensor_gather_start(tally, rows_ref, tensor)
    send_own(1)
    send_own(2)
    for keep in keeps:
        keep.wait()
    cot_state = tensor_gather_start(tally, cots_ref, tensor)
    tensor_gather_end(tally, rows_ref, tensor, rows_state)
    passed = []
    for place in range(3):
        full = full_refs[place]
        for step in range(1, count // 2):
            straight[place][step - 1].wait_recv()
            origin = lax.rem(shard + count - 2 * step, count)
            passed.append(tally.copy(full.at[origin], full.at[origin], shard=partner))
    tensor_gather_end(tally, cots_ref, tensor, cot_state)
    for arrived in beside + passed:
        arrived.wait_recv()
    tally.finish()


def middle_kernel(parts_ref, x_ref, bias_ref, gain_ref, shift_ref, hidden_ref, rows_ref,
                  landed, mixed, send, recv):
    tensor = lax.axis_index("tensor")
    greet([flip(tensor, 1), flip(tensor, 2)], [])
    tally = Tally(send, recv)
    state = tensor_sum_start(tally, parts_ref, landed, tensor)
    across = tensor_sum_pass(tally, parts_ref, landed, mixed, tensor, state)
    branch = tensor_sum_end(parts_ref, landed, tensor, state, across)
    hidden = x_ref[...].astype(F32) + branch + bias_ref[...]
    hidden_ref[...] = hidden
    rows_ref[tensor] = normalize(hidden, gain_ref[...], shift_ref[...])[0].astype(BF16)
    rows_state = tensor_gather_start(tally, rows_ref, tensor)
    tensor_gather_end(tally, rows_ref, tensor, rows_state)
    tally.finish()


def turn_kernel(parts_ref, hidden_ref, cot_ref, gain_ref, grad_ref, rows_ref, small_ref,
                landed, mixed, send, recv):
    tensor = lax.axis_index("tensor")
    greet([flip(tensor, 1), flip(tensor, 2)], [])
    tally = Tally(send, recv)
    state = tensor_sum_start(tally, parts_ref, landed, tensor)
    across = tensor_sum_pass(tally, parts_ref, landed, mixed, tensor, state)
    _, unit, inverse = normalize(hidden_ref[...], gain_ref[...], gain_ref[...])
    normed = tensor_sum_end(parts_ref, landed, tensor, state, across)
    grad_rows, grad_gain, grad_shift = norm_backward(normed, unit, inverse, gain_ref[...])
    cot = cot_ref[...].astype(F32)
    grad = cot + grad_rows
    grad_ref[...] = grad
    rows_ref[tensor] = grad.astype(BF16)
    rows_state = tensor_gather_start(tally, rows_ref, tensor)
    small_ref[0:1, :] = grad_gain.reshape(1, -1)
    small_ref[1:2, :] = grad_shift.reshape(1, -1)
    small_ref[2:3, :] = jnp.sum(grad, axis=0, keepdims=True)
    small_ref[3:4, :] = jnp.sum(cot, axis=0, keepdims=True)
    small_ref[4:8, :] = jnp.zeros((4, small_ref.shape[1]), F32)
    tensor_gather_end(tally, rows_ref, tensor, rows_state)
    tally.finish()


def shard_sum_start(tally, grads, ybufs, shard, count):
    half = count // 2
    place = lax.div(shard, 2)
    low = lax.rem(shard, 2)
    sent = []
    for step in list(range(1, half)) + [0]:
        pair = lax.rem(place + step, half)
        row = []
        for grad, ybuf in zip(grads, ybufs):
            row.append(
                tally.copy(grad.at[pair * 2 + 1 - low], ybuf.at[step], shard=flip(shard, 1))
            )
        sent.append((step, row))
    return sent


def shard_sum_pass(tally, grads, ybufs, zbufs, shard, count, sent):
    half = count // 2
    place = lax.div(shard, 2)
    low = lax.rem(shard, 2)
    across = []
    for step, row in sent:
        pair = lax.rem(place + step, half)
        for grad, ybuf, zbuf, arrived in zip(grads, ybufs, zbufs, row):
            arrived.wait_recv()
            if step:
                ybuf[step] = (
                    grad[pair * 2 + low].astype(F32) + ybuf[step].astype(F32)
                ).astype(BF16)
                across.append(
                    tally.copy(ybuf.at[step], zbuf.at[step], shard=pair * 2 + low)
                )
    return across


def shard_sum_end(grads, ybufs, zbufs, outs, shard, count, across):
    for arrived in across:
        arrived.wait_recv()
    for grad, ybuf, zbuf, out in zip(grads, ybufs, zbufs, outs):
        total = grad[shard].astype(F32) + ybuf[0].astype(F32)
        for step in range(1, count // 2):
            total = total + zbuf[step].astype(F32)
        out[...] = total


def last_kernel(count, two_ref, one_ref, hidden_ref, bias_ref, x_ref, gain_ref, grad_ref,
                small_ref, g0, g1, g2, output_ref, inputs_ref, o0, o1, o2, total_ref,
                landed2, mixed2, landed1, mixed1, y0, y1, y2, z0, z1, z2,
                mine, sums_t, sums_s, sums_g, send, recv):
    tensor, shard = lax.axis_index("tensor"), lax.axis_index("shard")
    near, far = flip(tensor, 1), flip(tensor, 2)
    partner = flip(shard, 1)
    peers = shard_peers_of(shard, count)
    greet([near, far, flip(near, 2)], peers)
    tally = Tally(send, recv)
    grads, ybufs, zbufs = (g0, g1, g2), (y0, y1, y2), (z0, z1, z2)
    sent = shard_sum_start(tally, grads, ybufs, shard, count)
    one_state = tensor_sum_start(tally, one_ref, landed1, tensor)
    two_state = tensor_sum_start(tally, two_ref, landed2, tensor)
    one_across = tensor_sum_pass(tally, one_ref, landed1, mixed1, tensor, one_state)
    two_across = tensor_sum_pass(tally, two_ref, landed2, mixed2, tensor, two_state)
    across = shard_sum_pass(tally, grads, ybufs, zbufs, shard, count, sent)
    _, unit, inverse = normalize(x_ref[...].astype(F32), gain_ref[...], gain_ref[...])
    normed = tensor_sum_end(one_ref, landed1, tensor, one_state, one_across)
    grad_rows, grad_gain, grad_shift = norm_backward(normed, unit, inverse, gain_ref[...])
    mine[0:6, :] = small_ref[0:6, :]
    mine[6:7, :] = grad_gain.reshape(1, -1)
    mine[7:8, :] = grad_shift.reshape(1, -1)
    half = count // 2
    first = tally.copy(mine, sums_s.at[0], shard=partner)
    inputs_ref[...] = grad_ref[...] + grad_rows
    first.wait_recv()
    sums_t[...] = mine[...] + sums_s[0]
    hops = [
        tally.copy(sums_t, sums_s.at[step], shard=lax.rem(shard + 2 * step, count))
        for step in range(1, half)
    ]
    branch = tensor_sum_end(two_ref, landed2, tensor, two_state, two_across)
    output_ref[...] = hidden_ref[...] + branch + bias_ref[...]
    for hop in hops:
        hop.wait_recv()
    slot_total = None
    for spot in range(half):
        step = lax.rem(lax.div(shard, 2) + half - spot, half)
        value = jnp.where(step == 0, sums_t[...], sums_s[step])
        slot_total = value if slot_total is None else slot_total + value
    sums_g[tensor] = slot_total
    spread = [
        tally.copy(sums_g.at[tensor], sums_g.at[tensor], tensor=peer)
        for peer in (near, far, flip(near, 2))
    ]
    shard_sum_end(grads, ybufs, zbufs, (o0, o1, o2), shard, count, across)
    for arrived in spread:
        arrived.wait_recv()
    total_ref[...] = sums_g[...]
    tally.finish()


def attend_kernel(heads, scale, qkv_ref, out_ref):
    length = qkv_ref.shape[0]
    width = heads * HD
    size = min(256, length)

    def block(step, carry):
        rows = pl.ds(pl.multiple_of(step * size, size), size)
        mixed = []
        for head in range(heads):
            query = qkv_ref[rows, head * HD:(head + 1) * HD]
            keys = qkv_ref[:, width + head * HD:width + (head + 1) * HD]
            values = qkv_ref[:, 2 * width + head * HD:2 * width + (head + 1) * HD]
            scores = lax.dot_general(
                query, keys, (((1,), (1,)), ((), ())), preferred_element_type=F32
            ) * scale
            exponent = jnp.exp(scores - jnp.max(scores, axis=1, keepdims=True))
            soft = (exponent * (1.0 / jnp.sum(exponent, axis=1, keepdims=True))).astype(BF16)
            mixed.append(jnp.dot(soft, values, preferred_element_type=F32))
        out_ref[rows, :] = jnp.concatenate(mixed, axis=1).astype(BF16)
        return carry

    lax.fori_loop(0, length // size, block, 0)


def attend_back_kernel(heads, scale, qkv_ref, grad_ref, low_ref, bias_ref, dq, dk, dv):
    length = qkv_ref.shape[0]
    width = heads * HD
    size = min(256, length)
    dk[...] = jnp.zeros_like(dk)
    dv[...] = jnp.zeros_like(dv)

    def block(step, carry):
        rows = pl.ds(pl.multiple_of(step * size, size), size)
        back = []
        for head in range(heads):
            query = qkv_ref[rows, head * HD:(head + 1) * HD]
            keys = qkv_ref[:, width + head * HD:width + (head + 1) * HD]
            values = qkv_ref[:, 2 * width + head * HD:2 * width + (head + 1) * HD]
            grad = grad_ref[rows, head * HD:(head + 1) * HD]
            scores = lax.dot_general(
                query, keys, (((1,), (1,)), ((), ())), preferred_element_type=F32
            ) * scale
            exponent = jnp.exp(scores - jnp.max(scores, axis=1, keepdims=True))
            soft = exponent * (1.0 / jnp.sum(exponent, axis=1, keepdims=True))
            grad_soft = lax.dot_general(
                grad, values, (((1,), (1,)), ((), ())), preferred_element_type=F32
            )
            inner = jnp.sum(grad_soft * soft, axis=1, keepdims=True)
            grad_scores = (soft * (grad_soft - inner) * scale).astype(BF16)
            back.append(jnp.dot(grad_scores, keys, preferred_element_type=F32))
            dk[head] += lax.dot_general(
                query, grad_scores, (((0,), (0,)), ((), ())), preferred_element_type=F32
            )
            dv[head] += lax.dot_general(
                grad, soft.astype(BF16), (((0,), (0,)), ((), ())), preferred_element_type=F32
            )
        dq[rows, :] = jnp.concatenate(back, axis=1)
        return carry

    lax.fori_loop(0, length // size, block, 0)
    key_rows = jnp.concatenate([dk[head] for head in range(heads)], axis=0).T
    value_rows = jnp.concatenate([dv[head] for head in range(heads)], axis=0).T
    query_rows = dq[...]
    low_ref[...] = jnp.concatenate([query_rows, key_rows, value_rows], axis=1).astype(BF16)
    bias_ref[...] = jnp.concatenate(
        [jnp.sum(query_rows, axis=0, keepdims=True), jnp.sum(value_rows, axis=0, keepdims=True)],
        axis=1,
    )


VM = pl.BlockSpec(memory_space=pltpu.VMEM)
HB = pl.BlockSpec(memory_space=pl.ANY)


def call(kernel, ins, outs, scratch, operands, name, collective=None):
    remote = collective is not None
    return pl.pallas_call(
        kernel,
        out_shape=list(outs),
        in_specs=ins,
        out_specs=[VM] * len(outs),
        scratch_shapes=scratch,
        compiler_params=pltpu.CompilerParams(
            vmem_limit_bytes=56 * 2**20,
            **(dict(collective_id=collective, has_side_effects=True) if remote else {}),
        ),
        name=name,
    )(*operands)


def dma(count):
    return [pltpu.SemaphoreType.DMA((count,)), pltpu.SemaphoreType.DMA((count,))]


def shape(dims, kind=BF16):
    return jax.ShapeDtypeStruct(tuple(dims), kind)


def shards(
    inputs, w_query, w_key, w_value, bias_query, bias_value, w_out, bias_out, gain_one,
    shift_one, gain_two, shift_two, w_up, bias_up, w_down, bias_down, cotangent,
):
    count, tensors = lax.axis_size("shard"), lax.axis_size("tensor")
    tensor = lax.axis_index("tensor")
    frames_here, width = inputs.shape
    length = frames_here * tensors
    cols = w_query.shape[1]
    heads = cols // HD
    units = w_up.shape[1]
    scale = 1.0 / math.sqrt(HD)
    rows = w_query.shape[0]
    padded = -(-rows // 16) * 16
    row = lambda vector: vector.reshape(1, -1)
    pad = lambda block: jnp.pad(block, ((0, padded - rows), (0, 0)))
    join = lambda blocks: blocks[:, :rows].reshape(count * rows, blocks.shape[2])
    split = lambda whole: jnp.pad(
        whole.reshape(count, rows, whole.shape[1]), ((0, 0), (0, padded - rows), (0, 0))
    )
    w_attend = jnp.concatenate([w_query, w_key, w_value, w_out.T], axis=1)
    wide = w_attend.shape[1]
    block = (tensors, frames_here, width)

    n_copies = 6 + 2 * 5 + 3 * count
    rows_one, cots, full_attend, full_up, full_down = call(
        functools.partial(gather_kernel, count),
        [VM] * 7,
        [shape(block), shape(block), shape((count, padded, wide)),
         shape((count, padded, units)), shape((count, padded, units))],
        dma(n_copies) + [pltpu.SemaphoreType.DMA((4,))],
        (inputs, row(gain_one), row(shift_one), cotangent, pad(w_attend), pad(w_up),
         pad(w_down.T)),
        "gather_all", 0,
    )
    rows_one = rows_one.reshape(length, width)
    cots = cots.reshape(length, width)
    full_attend, full_up, full_down = join(full_attend), join(full_up), join(full_down)
    full_qkv, full_out = full_attend[:, :3 * cols], full_attend[:, 3 * cols:]
    bias_qkv = jnp.concatenate([
        lax.dynamic_slice_in_dim(bias_query, tensor * cols, cols),
        jnp.zeros((cols,), F32),
        lax.dynamic_slice_in_dim(bias_value, tensor * cols, cols),
    ])
    up_bias = lax.dynamic_slice_in_dim(bias_up, tensor * units, units)
    qkv = (jnp.dot(rows_one, full_qkv, preferred_element_type=F32) + bias_qkv).astype(BF16)
    attended = call(
        functools.partial(attend_kernel, heads, scale), [VM],
        (shape((length, cols)),), [], (qkv,), "attend",
    )[0]
    partial_one = jnp.einsum("tc,dc->td", attended, full_out, preferred_element_type=F32)
    landing = [pltpu.VMEM((3, frames_here, width), BF16), pltpu.VMEM((frames_here, width), BF16)]
    hidden_state, rows_two = call(
        middle_kernel, [VM] * 5,
        [shape((frames_here, width), F32), shape(block)],
        landing + dma(10),
        (partial_one.astype(BF16).reshape(block), inputs, row(bias_out), row(gain_two),
         row(shift_two)),
        "middle", 1,
    )
    rows_two = rows_two.reshape(length, width)
    pre_act = jnp.dot(rows_two, full_up, preferred_element_type=F32) + up_bias
    activated = exact_gelu(pre_act).astype(BF16)
    grad_act = jnp.dot(cots, full_down, preferred_element_type=F32)
    grad_pre = jax.vjp(exact_gelu, pre_act)[1](grad_act)[0]
    grad_up_bias = jnp.sum(grad_pre, axis=0)
    grad_pre_low = grad_pre.astype(BF16)
    back_two = jnp.einsum("tf,df->td", grad_pre_low, full_up, preferred_element_type=F32)
    grad_hidden, rows_hidden, small = call(
        turn_kernel, [VM] * 4,
        [shape((frames_here, width), F32), shape(block), shape((8, width), F32)],
        landing + dma(10),
        (back_two.astype(BF16).reshape(block), hidden_state, cotangent, row(gain_two)),
        "turn", 2,
    )
    rows_hidden = rows_hidden.reshape(length, width)
    partial_two = jnp.einsum("tf,df->td", activated, full_down, preferred_element_type=F32)
    grad_down = jnp.einsum("td,tf->df", cots, activated, preferred_element_type=F32)
    grad_up = jnp.einsum("td,tf->df", rows_two, grad_pre_low, preferred_element_type=F32)
    grad_attended = jnp.dot(rows_hidden, full_out, preferred_element_type=F32).astype(BF16)
    low, bias_sums = call(
        functools.partial(attend_back_kernel, heads, scale), [VM] * 2,
        [shape((length, 3 * cols)), shape((1, 2 * cols), F32)],
        [pltpu.VMEM((length, cols), F32), pltpu.VMEM((heads, HD, length), F32),
         pltpu.VMEM((heads, HD, length), F32)],
        (qkv, grad_attended), "attend_back",
    )
    back_one = jnp.einsum("tc,dc->td", low, full_qkv, preferred_element_type=F32)
    grad_qkv = jnp.einsum("td,tc->dc", rows_one, low, preferred_element_type=F32).astype(BF16)
    grad_out = jnp.einsum("td,tc->dc", rows_hidden, attended, preferred_element_type=F32)
    grad_attend = jnp.concatenate([grad_qkv, grad_out.astype(BF16)], axis=1)
    small = small.at[4, :2 * cols].set(bias_sums[0]).at[5, :units].set(grad_up_bias)
    half = count // 2
    n_copies = 10 + 3 * (2 * half - 1) + half + 3
    output, grad_inputs, sum_attend, sum_up, sum_down, totals = call(
        functools.partial(last_kernel, count), [VM] * 11,
        [shape((frames_here, width), F32), shape((frames_here, width), F32),
         shape((padded, wide), F32), shape((padded, units), F32), shape((padded, units), F32),
         shape((tensors, 8, width), F32)],
        landing + landing
        + [pltpu.VMEM((half, padded, size), BF16) for size in (wide, units, units) * 2]
        + [pltpu.VMEM((8, width), F32), pltpu.VMEM((8, width), F32),
           pltpu.VMEM((half, 8, width), F32), pltpu.VMEM((tensors, 8, width), F32)]
        + dma(n_copies),
        (partial_two.astype(BF16).reshape(block), back_one.astype(BF16).reshape(block),
         hidden_state, row(bias_down), inputs, row(gain_one), grad_hidden, small,
         split(grad_attend), split(grad_up.astype(BF16)), split(grad_down.astype(BF16))),
        "last", 3,
    )
    sums = jnp.sum(totals, axis=0)
    sum_attend = sum_attend[:rows]
    return (
        output,
        grad_inputs,
        sum_attend[:, :cols],
        sum_attend[:, cols:2 * cols],
        sum_attend[:, 2 * cols:3 * cols],
        totals[:, 4, :cols].reshape(-1),
        totals[:, 4, cols:2 * cols].reshape(-1),
        sum_attend[:, 3 * cols:].T,
        sums[2],
        sums[6],
        sums[7],
        sums[0],
        sums[1],
        sum_up[:rows],
        totals[:, 5, :units].reshape(-1),
        sum_down[:rows].T,
        sums[3],
    )


def solution(mesh):
    placed = (
        P(("shard", "tensor"), None),
        P("shard", "tensor"),
        P("shard", "tensor"),
        P("shard", "tensor"),
        P(),
        P(),
        P("tensor", "shard"),
        P(),
        P(),
        P(),
        P(),
        P(),
        P("shard", "tensor"),
        P(),
        P("tensor", "shard"),
        P(),
        P(("shard", "tensor"), None),
    )
    return jax.shard_map(
        shards,
        mesh=mesh,
        in_specs=placed,
        out_specs=(
            P(("shard", "tensor"), None),
            P(("shard", "tensor"), None),
            P("shard", "tensor"),
            P("shard", "tensor"),
            P("shard", "tensor"),
            P(),
            P(),
            P("tensor", "shard"),
            P(),
            P(),
            P(),
            P(),
            P(),
            P("shard", "tensor"),
            P(),
            P("tensor", "shard"),
            P(),
        ),
        check_vma=False,
    )
```

time: 921 us -> 271 us (0.29)
  waiting for transfers between devices: 553 us -> 0 us
  Pallas kernels: 0 us -> 200 us
  blocking collectives: 169 us -> 0 us
  matrix products: 124 us -> 38.3 us
  other arithmetic: 29.9 us -> 3.16 us
  between operations: 16.3 us -> 0.87 us
    reduce_scatter x9 -> x0, waiting for transfers between devices: 403 us -> none  [the longest x1 72.4 us: shards(): lax.psum_scatter(grad_w_up, 'shard', scatter_dimension=0, tiled=True)]
    pallas_call x0 -> x6, Pallas kernels: none -> 200 us  [call(): pl.pallas_call(kernel, out_shape=list(outs), in_specs=ins, out_specs=[VM]...]
    all_gather x4 -> x0, blocking collectives: 127 us -> none  [the longest x1 32.9 us: shards(): lax.all_gather(w_out, 'shard', axis=1, tiled=True)]
    all_gather x6 -> x0, waiting for transfers between devices: 107 us -> none  [the longest x1 39.1 us: shards(): lax.all_gather(w_down, 'shard', axis=1, tiled=True)]
    dot_general x31 -> x12, matrix products: 121 us -> 38.3 us  [the longest x1 8.3 us: shards(): grad_act = jnp.dot(cots, full_down, preferred_element_type=F32)]
    psum x1 -> x0, blocking collectives: 42.5 us -> none  [shards(): lax.psum((full_query_bias, full_value_bias, grad_bias_out, grad_gain_one,...]
    unnamed x17 -> x0, waiting for transfers between devices: 42.3 us -> none
    reduce_sum x11 -> x1, other arithmetic: 16.3 us -> 0.9 us  [shards(): sums = jnp.sum(totals, axis=0)]
  transfers between devices with their start and end apart: 16 -> 0, of which waited for: 15 -> 0; matrix products, arithmetic and copies ran while one was open for 5% -> 0% of each run, Pallas kernels for 0% -> 0%
where the time goes in v1:
time: 271 us; the launch traced here: 270 us
  Pallas kernels  200 us (74%)
  matrix products  38.3 us (14%)
  local copies, waits for them, and re-layouts  27.4 us (10%)
  other arithmetic  3.16 us (1%)
    pallas_call x6, Pallas kernels, call(): pl.pallas_call(kernel, out_shape=list(outs), in_specs=ins, out_specs=[VM]...  200 us
    dot_general x1, matrix products, shards(): grad_act = jnp.dot(cots, full_down, preferred_element_type=F32)  8.3 us
    reshape x6, local copies, waits for them, and re-layouts, shards(): row = lambda vector: vector.reshape(1, -1)  7.6 us
    unnamed x28, local copies, waits for them, and re-layouts  6.04 us

profile of v1, /device:TPU:0, one launch (start us, length us, event | category | flops | bytes accessed | tf_op | source)
XLA Modules:
  0.0 269.8 jit_solution(18271801656204858930)
XLA Ops:
  11.5 1.6 pad_maximum_fusion.1.refs_4_
  13.1 57.4 %gather_all.1 = (bf16[4,256,768]{2,1,0:T(8,128)(2,1)}, bf16[4,256,768]{2,1,0:T(8,128)(2,1)}, bf16[8,96,768]{2,1,0:T(8,128)(2,1)}, bf16[8,96,768]{2,1,0:T(8,128)(2,1)}, bf16[8,96,768]{2,1,0:T(8,128)(2,1)}) custom-call(bf16[256,768]{1,0:T(8,128)(2,1)} %x_ref.3, f32[1,768]{1,0:T(1,128)} %reshape.152.refs_1_.gain_ref, f32[1,768]{1,0:T(1,128)} %reshape.153.refs_2_, ...), custom_call_target="tpu_custom_call" | custom-call | tf_op jit(solution)/shard_map/gather_all/pallas_call | solution.py:402
  70.5 4.2 %add_convert_fusion.qkv_ref = bf16[1024,576]{1,0:T(8,128)(2,1)} fusion(bf16[1024,768]{1,0:T(8,128)(2,1)} %bitcast.57, f32[576]{0:T(1024)S(1)} %pad_maximum_fusion.2, bf16[768,768]{1,0:T(8,128)(2,1)} %bitcast.49), kind=kOutput, calls=%fused_computation.17 | convolution fusion | flops 907149312 | bytes 3737856 | tf_op jit(solution)/shard_map/dot_general | solution.py:469
  74.8 10.9 %attend.1 = bf16[1024,192]{1,0:T(8,128)(2,1)} custom-call(bf16[1024,576]{1,0:T(8,128)(2,1)} %add_convert_fusion.qkv_ref), custom_call_target="tpu_custom_call" | custom-call | tf_op jit(solution)/shard_map/attend/pallas_call | solution.py:402
  85.7 2.9 %convolution_convert_fusion.3 = bf16[1024,768]{1,0:T(8,128)(2,1)} fusion(bf16[1024,192]{1,0:T(8,128)(2,1)} %attend.1, bf16[768,768]{1,0:T(8,128)(2,1)S(1)} %bitcast.50), kind=kOutput, calls=%fused_computation.21 | convolution fusion | flops 302776320 | bytes 2359296 | tf_op jit(solution)/shard_map/tc,dc->td/dot_general | solution.py:474
  88.6 27.9 %middle.1 = (f32[256,768]{1,0:T(8,128)}, bf16[4,256,768]{2,1,0:T(8,128)(2,1)}) custom-call(bf16[4,256,768]{2,1,0:T(8,128)(2,1)} %bitcast.40, bf16[256,768]{1,0:T(8,128)(2,1)} %x_ref.3, f32[1,768]{1,0:T(1,128)} %reshape.157.bias_ref, f32[1,768]{1,0:T(1,128)} %reshape.158.gain_ref, f32[1,768]{1,0:T(1,128)} %reshape.159.shift_ref), custom_call_target="tpu_custom_call" | custom-call | tf_op jit(solution)/shard_map/middle/pallas_call | solution.py:402
  116.5 2.9 %fusion.14 = f32[1024,768]{1,0:T(8,128)S(1)} fusion(bf16[1024,768]{1,0:T(8,128)(2,1)} %bitcast.61, bf16[768,768]{1,0:T(8,128)(2,1)S(1)} %bitcast.63), kind=kOutput, calls=%fused_computation.46 | convolution fusion | flops 1207959552 | bytes 5898240 | tf_op jit(solution)/shard_map/dot_general | solution.py:485
  119.5 8.3 %fusion.12 = (f32[768]{0:T(1024)S(1)}, bf16[1024,768]{1,0:T(8,128)(2,1)S(1)}, f32[1024,768]{1,0:T(8,128)S(1)}) fusion(f32[1024,768]{1,0:T(8,128)S(1)} %fusion.14, f32[768]{0:T(1024)S(1)} %dynamic_slice.11, bf16[1024,768]{1,0:T(8,128)(2,1)S(1)} %bitcast.59, bf16[768,768]{1,0:T(8,128)(2,1)S(1)} %bitcast.65), kind=kOutput, calls=%fused_computation.45 | convolution fusion | flops 1266154752 | bytes 10622976 | tf_op jit(solution)/shard_map/dot_general | solution.py:487
  127.8 2.6 convolution_convert_fusion.5
  130.8 2.5 convolution_convert_fusion.4
  133.4 2.6 convolution_convert_fusion.2
  136.0 2.6 convolution_convert_fusion.1
  138.5 27.3 %turn.1 = (f32[256,768]{1,0:T(8,128)}, bf16[4,256,768]{2,1,0:T(8,128)(2,1)}, f32[8,768]{1,0:T(8,128)}) custom-call(bf16[4,256,768]{2,1,0:T(8,128)(2,1)} %bitcast.46, f32[256,768]{1,0:T(8,128)} %get-tuple-element.65.hidden_ref, bf16[256,768]{1,0:T(8,128)(2,1)} %cot_ref.1, f32[1,768]{1,0:T(1,128)} %reshape.158.gain_ref), custom_call_target="tpu_custom_call" | custom-call | tf_op jit(solution)/shard_map/turn/pallas_call | solution.py:402
  165.9 2.0 convolution_convert_fusion.8
  169.7 16.0 %attend_back.1 = (bf16[1024,576]{1,0:T(8,128)(2,1)}, f32[1,384]{1,0:T(1,128)}) custom-call(bf16[1024,576]{1,0:T(8,128)(2,1)} %add_convert_fusion.qkv_ref, bf16[1024,192]{1,0:T(8,128)(2,1)} %copy.41.grad_ref), custom_call_target="tpu_custom_call" | custom-call | tf_op jit(solution)/shard_map/attend_back/pallas_call | solution.py:402
  185.7 2.9 %convolution_convert_fusion.6 = bf16[768,576]{0,1:T(8,128)(2,1)S(1)} fusion(bf16[1024,768]{1,0:T(8,128)(2,1)} %bitcast.58, bf16[1024,576]{1,0:T(8,128)(2,1)} %get-tuple-element.67), kind=kOutput, calls=%fused_computation.24 | convolution fusion | flops 906412032 | bytes 3637248 | tf_op jit(solution)/shard_map/td,tc->dc/dot_general | solution.py:512
  188.6 1.4 scatter.6
  190.0 1.3 scatter.9.small_ref
  191.4 1.5 copy.42
  192.9 3.9 %convolution_convert_fusion = bf16[1024,768]{1,0:T(8,128)(2,1)} fusion(bf16[1024,576]{1,0:T(8,128)(2,1)} %get-tuple-element.67, bf16[768,768]{1,0:T(8,128)(2,1)S(1)} %bitcast.52), kind=kOutput, calls=%fused_computation.18 | convolution fusion | flops 906756096 | bytes 3735552 | tf_op jit(solution)/shard_map/tc,dc->td/dot_general | solution.py:511
  196.8 60.7 %last.1 = (f32[256,768]{1,0:T(8,128)}, f32[256,768]{1,0:T(8,128)}, f32[96,768]{1,0:T(8,128)}, f32[96,768]{1,0:T(8,128)}, f32[96,768]{1,0:T(8,128)}, /*index=5*/f32[4,8,768]{2,1,0:T(8,128)}) custom-call(bf16[4,256,768]{2,1,0:T(8,128)(2,1)} %bitcast.42, bf16[4,256,768]{2,1,0:T(8,128)(2,1)} %bitcast.43, f32[256,768]{1,0:T(8,128)} %get-tuple-element.65.hidden_ref, ...), custom_call_target="tpu_custom_call" | custom-call | tf_op jit(solution)/shard_map/last/pallas_call | solution.py:402
  259.8 1.5 slice.92
  262.9 1.8 slice_bitcast_fusion
  265.5 2.1 copy.51
  (48 shorter events, 20.2 us)
Async XLA Ops:
  70.5 15.2 %copy-start.3 = (bf16[8,96,768]{2,1,0:T(8,128)(2,1)S(1)}, bf16[8,96,768]{2,1,0:T(8,128)(2,1)}, u32[]{:S(2)}) copy-start(bf16[8,96,768]{2,1,0:T(8,128)(2,1)} %get-tuple-element.60) | copy-start | bytes 3538948
  74.8 41.7 %copy-start.9 = (bf16[8,96,768]{2,1,0:T(8,128)(2,1)S(1)}, bf16[8,96,768]{2,1,0:T(8,128)(2,1)}, u32[]{:S(2)}) copy-start(bf16[8,96,768]{2,1,0:T(8,128)(2,1)} %get-tuple-element.62) | copy-start | bytes 3538948
  116.5 3.0 %copy-start.7 = (bf16[4,256,768]{2,1,0:T(8,128)(2,1)S(1)}, bf16[4,256,768]{2,1,0:T(8,128)(2,1)}, u32[]{:S(2)}) copy-start(bf16[4,256,768]{2,1,0:T(8,128)(2,1)} %get-tuple-element.64) | copy-start | bytes 4718596
  116.5 3.0 %copy-start.10 = (bf16[8,96,768]{2,1,0:T(8,128)(2,1)S(1)}, bf16[8,96,768]{2,1,0:T(8,128)(2,1)}, u32[]{:S(2)}) copy-start(bf16[8,96,768]{2,1,0:T(8,128)(2,1)} %get-tuple-element.63) | copy-start | bytes 3538948
  119.5 8.3 %copy-start.8 = (bf16[4,256,768]{2,1,0:T(8,128)(2,1)S(1)}, bf16[4,256,768]{2,1,0:T(8,128)(2,1)}, u32[]{:S(2)}) copy-start(bf16[4,256,768]{2,1,0:T(8,128)(2,1)} %get-tuple-element.61) | copy-start | bytes 4718596
  136.0 29.9 %copy-start = (bf16[1024,192]{1,0:T(8,128)(2,1)S(1)}, bf16[1024,192]{1,0:T(8,128)(2,1)}, u32[]{:S(2)}) copy-start(bf16[1024,192]{1,0:T(8,128)(2,1)} %attend.1) | copy-start | bytes 1179652
  165.8 2.1 copy-start.1
  185.7 2.9 %copy-start.6 = (f32[1,384]{1,0:T(1,128)S(1)}, f32[1,384]{1,0:T(1,128)}, u32[]{:S(2)}) copy-start(f32[1,384]{1,0:T(1,128)} %get-tuple-element.70) | copy-start | bytes 4612
  257.5 10.1 %copy-start.2 = (f32[256,768]{1,0:T(8,128)S(1)}, f32[256,768]{1,0:T(8,128)}, u32[]{:S(2)}) copy-start(f32[256,768]{1,0:T(8,128)} %get-tuple-element.147) | copy-start | bytes 2359300
  257.5 10.9 %copy-start.5 = (f32[96,768]{1,0:T(8,128)S(1)}, f32[96,768]{1,0:T(8,128)}, u32[]{:S(2)}) copy-start(f32[96,768]{1,0:T(8,128)} %get-tuple-element.159) | copy-start | bytes 884740
  257.5 11.6 %copy-start.4 = (f32[96,768]{1,0:T(8,128)S(1)}, f32[96,768]{1,0:T(8,128)}, u32[]{:S(2)}) copy-start(f32[96,768]{1,0:T(8,128)} %get-tuple-element.76) | copy-start | bytes 884740

commit v2 on v1

v2 whole, which is shorter than its diff:
```python
import functools
import math

import jax
import jax.numpy as jnp
from jax import lax
from jax.experimental import pallas as pl
from jax.experimental.pallas import tpu as pltpu
from jax.sharding import PartitionSpec as P

HD = 64
MESH = pl.DeviceIdType.MESH
F32 = jnp.float32
BF16 = jnp.bfloat16

epsilon = 1e-05


def normalize(matrix, gain_vec, shift_vec):
    center = matrix - jnp.mean(matrix, axis=1, keepdims=True)
    inverse = lax.rsqrt(jnp.mean(center * center, axis=1, keepdims=True) + epsilon)
    unit_rows = center * inverse
    return (unit_rows * gain_vec + shift_vec, unit_rows, inverse)


def norm_backward(grad_normed, unit_rows, inverse, gain_vec):
    grad_unit = grad_normed * gain_vec
    first_mean = jnp.mean(grad_unit, axis=1, keepdims=True)
    second_mean = jnp.mean(grad_unit * unit_rows, axis=1, keepdims=True)
    grad_rows = inverse * (grad_unit - first_mean - unit_rows * second_mean)
    return (grad_rows, jnp.sum(grad_normed * unit_rows, axis=0), jnp.sum(grad_normed, axis=0))


def exact_gelu(values):
    return jax.nn.gelu(values, approximate=False)


def flip(index, bit):
    return index + bit - 2 * bit * lax.rem(lax.div(index, bit), 2)


def greet(tensor_peers, shard_peers):
    barrier = pltpu.get_barrier_semaphore()
    for peer in tensor_peers:
        pl.semaphore_signal(barrier, inc=1, device_id={"tensor": peer}, device_id_type=MESH)
    for peer in shard_peers:
        pl.semaphore_signal(barrier, inc=1, device_id={"shard": peer}, device_id_type=MESH)
    pl.semaphore_wait(barrier, len(tensor_peers) + len(shard_peers))


def shard_peers_of(me, count):
    return [flip(me, 1)] + [lax.rem(me + 2 * step, count) for step in range(1, count // 2)]


class Tally:
    def __init__(self, send, recv):
        self.send, self.recv, self.used, self.sent = send, recv, 0, []

    def copy(self, source, target, **peer):
        slot = self.used
        self.used += 1
        made = pltpu.make_async_remote_copy(
            src_ref=source,
            dst_ref=target,
            send_sem=self.send.at[slot],
            recv_sem=self.recv.at[slot],
            device_id=peer,
            device_id_type=MESH,
        )
        made.start()
        self.sent.append(made)
        return made

    def finish(self):
        for made in self.sent:
            made.wait_send()


def halves(rows, parts=2):
    size = rows // parts
    return [pl.ds(part * size, size) for part in range(parts)]


def tensor_gather_start(tally, blocks, tensor):
    rows = blocks.shape[1]
    far = [
        tally.copy(blocks.at[tensor, cut], blocks.at[tensor, cut], tensor=flip(tensor, 2))
        for cut in halves(rows)
    ]
    near = [tally.copy(blocks.at[tensor], blocks.at[tensor], tensor=flip(tensor, 1))]
    return far, near


def tensor_gather_end(tally, blocks, tensor, state):
    far, near = state
    rows = blocks.shape[1]
    other = flip(tensor, 2)
    for arrived, cut in zip(far, halves(rows)):
        arrived.wait_recv()
        near.append(
            tally.copy(blocks.at[other, cut], blocks.at[other, cut], tensor=flip(tensor, 1))
        )
    for arrived in near:
        arrived.wait_recv()


def sum_start_pass(tally, parts, landed, tensor):
    sibling = flip(tensor, 1)
    return [
        tally.copy(parts.at[flip(sibling, 2), cut], landed.at[1, cut], tensor=sibling)
        for cut in halves(parts.shape[1])
    ]


def sum_start_own(tally, parts, landed, tensor):
    sibling = flip(tensor, 1)
    return tally.copy(parts.at[sibling], landed.at[0], tensor=sibling)


def tensor_sum_start(tally, parts, landed, tensor):
    passing = sum_start_pass(tally, parts, landed, tensor)
    return passing, sum_start_own(tally, parts, landed, tensor)


def tensor_sum_pass(tally, parts, landed, mixed, tensor, state):
    far = flip(tensor, 2)
    rows = parts.shape[1]
    across = []
    for arrived, cut in zip(state[0], halves(rows)):
        arrived.wait_recv()
        mixed[cut, :] = (parts[far, cut, :].astype(F32) + landed[1, cut, :].astype(F32)).astype(
            BF16
        )
        across.append(tally.copy(mixed.at[cut], landed.at[2, cut], tensor=far))
    return across


def tensor_sum_end(parts, landed, tensor, state, across):
    state[1].wait_recv()
    for arrived in across:
        arrived.wait_recv()
    return parts[tensor].astype(F32) + landed[0].astype(F32) + landed[2].astype(F32)


def soft_rows(query, keys, scale):
    scores = lax.dot_general(
        query, keys, (((1,), (1,)), ((), ())), preferred_element_type=F32
    ) * scale
    exponent = jnp.exp(scores - jnp.max(scores, axis=1, keepdims=True))
    return exponent * (1.0 / jnp.sum(exponent, axis=1, keepdims=True))


def head_of(ref, rows, head, part, width):
    begin = part * width + head * HD
    return ref[rows, begin:begin + HD]


def front_kernel(count, heads, kept, scale, x_ref, vec_ref, bias_ref, cot_ref, w0, w1, w2,
                 rows_ref, cots_ref, up_ref, down_ref, qkv_w, out_w, qkv_ref, attended_ref,
                 hidden_ref, two_ref, attend_full, parts, landed, mixed, send, recv, local):
    tensor, shard = lax.axis_index("tensor"), lax.axis_index("shard")
    partner = flip(shard, 1)
    peers = shard_peers_of(shard, count)
    greet([flip(tensor, 1), flip(tensor, 2)], peers)
    tally = Tally(send, recv)
    w_refs, full_refs = (w0, w1, w2), (attend_full, up_ref, down_ref)
    keeps = []
    for place, (w_ref, full) in enumerate(zip(w_refs, full_refs)):
        keeps.append(pltpu.make_async_copy(w_ref, full.at[shard], local.at[place]))
    keeps.append(pltpu.make_async_copy(cot_ref, cots_ref.at[tensor], local.at[3]))
    straight, beside = [], []

    def send_own(place):
        w_ref, full = w_refs[place], full_refs[place]
        straight.append([tally.copy(w_ref, full.at[shard], shard=peer) for peer in peers[1:]])
        beside.append(tally.copy(w_ref, full.at[shard], shard=partner))

    passed = [[], [], []]

    def forward(place):
        full = full_refs[place]
        for step in range(1, count // 2):
            straight[place][step - 1].wait_recv()
            origin = lax.rem(shard + count - 2 * step, count)
            passed[place].append(tally.copy(full.at[origin], full.at[origin], shard=partner))

    send_own(0)
    gain_one, shift_one = vec_ref[0:1, :], vec_ref[1:2, :]
    rows_ref[tensor] = normalize(x_ref[...].astype(F32), gain_one, shift_one)[0].astype(BF16)
    rows_state = tensor_gather_start(tally, rows_ref, tensor)
    for keep in keeps:
        keep.start()
    send_own(1)
    send_own(2)
    for keep in keeps:
        keep.wait()
    tensor_gather_end(tally, rows_ref, tensor, rows_state)
    cot_state = tensor_gather_start(tally, cots_ref, tensor)
    forward(0)
    for arrived in beside[:1] + passed[0]:
        arrived.wait_recv()
    width = heads * HD
    for place in range(count):
        into = slice(place * kept, (place + 1) * kept)
        qkv_w[into, :] = attend_full[place, :kept, :3 * width]
        out_w[into, :] = attend_full[place, :kept, 3 * width:]
    size = rows_ref.shape[1]

    def project(step, carry):
        rows = pl.ds(pl.multiple_of(step * size, size), size)
        qkv_ref[rows, :] = (
            jnp.dot(rows_ref[step], qkv_w[...], preferred_element_type=F32) + bias_ref[...]
        ).astype(BF16)
        return carry

    lax.fori_loop(0, rows_ref.shape[0], project, 0)
    everything = slice(None)

    def attend(owner):
        rows = pl.ds(pl.multiple_of(owner * size, size), size)
        blended = []
        for head in range(heads):
            soft = soft_rows(
                head_of(qkv_ref, rows, head, 0, width),
                head_of(qkv_ref, everything, head, 1, width), scale,
            ).astype(BF16)
            values = head_of(qkv_ref, everything, head, 2, width)
            blended.append(jnp.dot(soft, values, preferred_element_type=F32))
        attended = jnp.concatenate(blended, axis=1).astype(BF16)
        attended_ref[rows, :] = attended
        parts[owner] = lax.dot_general(
            attended, out_w[...], (((1,), (1,)), ((), ())), preferred_element_type=F32
        ).astype(BF16)

    sibling, far = flip(tensor, 1), flip(tensor, 2)
    attend(flip(sibling, 2))
    passing = sum_start_pass(tally, parts, landed, tensor)
    attend(far)
    across = tensor_sum_pass(tally, parts, landed, mixed, tensor, (passing, None))
    attend(sibling)
    own = sum_start_own(tally, parts, landed, tensor)
    attend(tensor)
    forward(1)
    branch = tensor_sum_end(parts, landed, tensor, (passing, own), across)
    hidden = x_ref[...].astype(F32) + branch + vec_ref[2:3, :]
    hidden_ref[...] = hidden
    two_ref[tensor] = normalize(hidden, vec_ref[3:4, :], vec_ref[4:5, :])[0].astype(BF16)
    two_state = tensor_gather_start(tally, two_ref, tensor)
    forward(2)
    tensor_gather_end(tally, cots_ref, tensor, cot_state)
    tensor_gather_end(tally, two_ref, tensor, two_state)
    for arrived in beside[1:] + passed[1] + passed[2]:
        arrived.wait_recv()
    tally.finish()


def shard_sum_start(tally, grads, ybufs, shard, count):
    half = count // 2
    place = lax.div(shard, 2)
    low = lax.rem(shard, 2)
    sent = []
    for step in list(range(1, half)) + [0]:
        pair = lax.rem(place + step, half)
        row = []
        for grad, ybuf in zip(grads, ybufs):
            row.append(
                tally.copy(grad.at[pair * 2 + 1 - low], ybuf.at[step], shard=flip(shard, 1))
            )
        sent.append((step, row))
    return sent


def shard_sum_pass(tally, grads, ybufs, zbufs, shard, count, sent):
    half = count // 2
    place = lax.div(shard, 2)
    low = lax.rem(shard, 2)
    across = []
    for step, row in sent:
        pair = lax.rem(place + step, half)
        for grad, ybuf, zbuf, arrived in zip(grads, ybufs, zbufs, row):
            arrived.wait_recv()
            if step:
                ybuf[step] = (
                    grad[pair * 2 + low].astype(F32) + ybuf[step].astype(F32)
                ).astype(BF16)
                across.append(
                    tally.copy(ybuf.at[step], zbuf.at[step], shard=pair * 2 + low)
                )
    return across


def shard_sum_end(grads, ybufs, zbufs, outs, shard, count, across):
    for arrived in across:
        arrived.wait_recv()
    for grad, ybuf, zbuf, out in zip(grads, ybufs, zbufs, outs):
        total = grad[shard].astype(F32) + ybuf[0].astype(F32)
        for step in range(1, count // 2):
            total = total + zbuf[step].astype(F32)
        out[...] = total


def back_kernel(count, heads, kept, scale, back_ref, two_ref, hidden_ref, cot_ref, x_ref,
                vec_ref, qkv_ref, attended_ref, rows_ref, qkv_w, out_w, up_bias, g1, g2,
                output_ref, inputs_ref, o0, o1, o2, total_ref,
                landed0, mixed0, landed2, mixed2, landed1, mixed1, y0, y1, y2, z0, z1, z2,
                grad_ref, rows_hidden, grad_att, dq, dk, dv, low, one_ref, acc_qkv, acc_out, g0,
                mine, sums_t, sums_s, sums_g, send, recv):
    tensor, shard = lax.axis_index("tensor"), lax.axis_index("shard")
    near, far = flip(tensor, 1), flip(tensor, 2)
    partner = flip(shard, 1)
    peers = shard_peers_of(shard, count)
    greet([near, far, flip(near, 2)], peers)
    tally = Tally(send, recv)
    width = heads * HD
    half = count // 2
    size = rows_ref.shape[1]
    blocks = rows_ref.shape[0]
    length = size * blocks
    state = tensor_sum_start(tally, back_ref, landed0, tensor)
    feed, feed_y, feed_z = (g1, g2), (y1, y2), (z1, z2)
    feed_sent = shard_sum_start(tally, feed, feed_y, shard, count)
    across = tensor_sum_pass(tally, back_ref, landed0, mixed0, tensor, state)
    gain_one, gain_two = vec_ref[0:1, :], vec_ref[3:4, :]
    _, unit, inverse = normalize(hidden_ref[...], gain_two, gain_two)
    normed = tensor_sum_end(back_ref, landed0, tensor, state, across)
    grad_rows, grad_gain, grad_shift = norm_backward(normed, unit, inverse, gain_two)
    cot = cot_ref[...].astype(F32)
    grad = cot + grad_rows
    grad_ref[...] = grad
    rows_hidden[tensor] = grad.astype(BF16)
    rows_state = tensor_gather_start(tally, rows_hidden, tensor)
    mine[0:1, :] = grad_gain.reshape(1, -1)
    mine[1:2, :] = grad_shift.reshape(1, -1)
    mine[2:3, :] = jnp.sum(grad, axis=0, keepdims=True)
    mine[3:4, :] = jnp.sum(cot, axis=0, keepdims=True)
    mine[5:6, :] = up_bias[...]
    dk[...] = jnp.zeros_like(dk)
    dv[...] = jnp.zeros_like(dv)
    acc_qkv[...] = jnp.zeros_like(acc_qkv)
    acc_out[...] = jnp.zeros_like(acc_out)
    tensor_gather_end(tally, rows_hidden, tensor, rows_state)
    two_state = tensor_sum_start(tally, two_ref, landed2, tensor)
    feed_across = shard_sum_pass(tally, feed, feed_y, feed_z, shard, count, feed_sent)
    everything = slice(None)
    turned = (((0,), (0,)), ((), ()))
    crossed = (((1,), (1,)), ((), ()))

    def prepare(step, carry):
        rows = pl.ds(pl.multiple_of(step * size, size), size)
        grads = rows_hidden[step]
        grad_att[rows, :] = jnp.dot(grads, out_w[...], preferred_element_type=F32).astype(BF16)
        acc_out[...] += lax.dot_general(
            grads, attended_ref[rows, :], turned, preferred_element_type=F32
        )
        return carry

    lax.fori_loop(0, blocks, prepare, 0)
    two_across = tensor_sum_pass(tally, two_ref, landed2, mixed2, tensor, two_state)

    def block(step, carry):
        rows = pl.ds(pl.multiple_of(step * size, size), size)
        back = []
        for head in range(heads):
            query = head_of(qkv_ref, rows, head, 0, width)
            keys = head_of(qkv_ref, everything, head, 1, width)
            values = head_of(qkv_ref, everything, head, 2, width)
            grad = grad_att[rows, head * HD:(head + 1) * HD]
            soft = soft_rows(query, keys, scale)
            grad_soft = lax.dot_general(grad, values, crossed, preferred_element_type=F32)
            inner = jnp.sum(grad_soft * soft, axis=1, keepdims=True)
            grad_scores = (soft * (grad_soft - inner) * scale).astype(BF16)
            back.append(jnp.dot(grad_scores, keys, preferred_element_type=F32))
            dk[head] += lax.dot_general(query, grad_scores, turned, preferred_element_type=F32)
            dv[head] += lax.dot_general(
                grad, soft.astype(BF16), turned, preferred_element_type=F32
            )
        dq[rows, :] = jnp.concatenate(back, axis=1)
        return carry

    lax.fori_loop(0, blocks, block, 0)
    key_rows = jnp.concatenate([dk[head] for head in range(heads)], axis=0).T
    value_rows = jnp.concatenate([dv[head] for head in range(heads)], axis=0).T
    query_rows = dq[...]
    low[...] = jnp.concatenate([query_rows, key_rows, value_rows], axis=1).astype(BF16)
    mine[4:5, :] = jnp.concatenate(
        [jnp.sum(query_rows, axis=0, keepdims=True), jnp.sum(value_rows, axis=0, keepdims=True),
         jnp.zeros((1, mine.shape[1] - 2 * width), F32)],
        axis=1,
    )

    def spread_back(owner):
        rows = pl.ds(pl.multiple_of(owner * size, size), size)
        one_ref[owner] = lax.dot_general(
            low[rows, :], qkv_w[...], crossed, preferred_element_type=F32
        ).astype(BF16)

    spread_back(flip(near, 2))
    one_pass = sum_start_pass(tally, one_ref, landed1, tensor)
    spread_back(far)
    spread_back(near)
    one_state = (one_pass, sum_start_own(tally, one_ref, landed1, tensor))
    one_across = tensor_sum_pass(tally, one_ref, landed1, mixed1, tensor, one_state)
    spread_back(tensor)

    def weights(step, carry):
        rows = pl.ds(pl.multiple_of(step * size, size), size)
        acc_qkv[...] += lax.dot_general(
            rows_ref[step], low[rows, :], turned, preferred_element_type=F32
        )
        return carry

    lax.fori_loop(0, blocks, weights, 0)
    if kept != g0.shape[1]:
        g0[...] = jnp.zeros_like(g0)
    for place in range(count):
        part = slice(place * kept, (place + 1) * kept)
        g0[place, :kept, :] = jnp.concatenate([acc_qkv[part, :], acc_out[part, :]], axis=1).astype(
            BF16
        )
    sent = shard_sum_start(tally, (g0,), (y0,), shard, count)
    _, unit, inverse = normalize(x_ref[...].astype(F32), gain_one, gain_one)
    normed = tensor_sum_end(one_ref, landed1, tensor, one_state, one_across)
    grad_rows, grad_gain, grad_shift = norm_backward(normed, unit, inverse, gain_one)
    mine[6:7, :] = grad_gain.reshape(1, -1)
    mine[7:8, :] = grad_shift.reshape(1, -1)
    first = tally.copy(mine, sums_s.at[0], shard=partner)
    inputs_ref[...] = grad_ref[...] + grad_rows
    attend_across = shard_sum_pass(tally, (g0,), (y0,), (z0,), shard, count, sent)
    first.wait_recv()
    sums_t[...] = mine[...] + sums_s[0]
    hops = [
        tally.copy(sums_t, sums_s.at[step], shard=lax.rem(shard + 2 * step, count))
        for step in range(1, half)
    ]
    branch = tensor_sum_end(two_ref, landed2, tensor, two_state, two_across)
    output_ref[...] = hidden_ref[...] + branch + vec_ref[5:6, :]
    shard_sum_end(feed, feed_y, feed_z, (o1, o2), shard, count, feed_across)
    for hop in hops:
        hop.wait_recv()
    slot_total = None
    for spot in range(half):
        step = lax.rem(lax.div(shard, 2) + half - spot, half)
        value = jnp.where(step == 0, sums_t[...], sums_s[step])
        slot_total = value if slot_total is None else slot_total + value
    sums_g[tensor] = slot_total
    spread = [
        tally.copy(sums_g.at[tensor], sums_g.at[tensor], tensor=peer)
        for peer in (near, far, flip(near, 2))
    ]
    shard_sum_end((g0,), (y0,), (z0,), (o0,), shard, count, attend_across)
    for arrived in spread:
        arrived.wait_recv()
    total_ref[...] = sums_g[...]
    tally.finish()


def finish_kernel(cols, kept, output_in, inputs_in, attend_in, up_in, down_in, total_in,
                  output_ref, inputs_ref, query_ref, key_ref, value_ref, out_ref, up_ref,
                  down_ref, sum_ref):
    output_ref[...] = output_in[...]
    inputs_ref[...] = inputs_in[...]
    query_ref[...] = attend_in[:kept, :cols]
    key_ref[...] = attend_in[:kept, cols:2 * cols]
    value_ref[...] = attend_in[:kept, 2 * cols:3 * cols]
    out_ref[...] = attend_in[:kept, 3 * cols:].T
    up_ref[...] = up_in[:kept, :]
    down_ref[...] = down_in[:kept, :].T
    sum_ref[...] = jnp.sum(total_in[...], axis=0)


VM = pl.BlockSpec(memory_space=pltpu.VMEM)
HB = pl.BlockSpec(memory_space=pl.ANY)


def call(kernel, ins, outs, scratch, operands, name, collective=None):
    remote = collective is not None
    return pl.pallas_call(
        kernel,
        out_shape=list(outs),
        in_specs=ins,
        out_specs=[VM] * len(outs),
        scratch_shapes=scratch,
        compiler_params=pltpu.CompilerParams(
            vmem_limit_bytes=56 * 2**20,
            **(dict(collective_id=collective, has_side_effects=True) if remote else {}),
        ),
        name=name,
    )(*operands)


def dma(count):
    return [pltpu.SemaphoreType.DMA((count,)), pltpu.SemaphoreType.DMA((count,))]


def shape(dims, kind=BF16):
    return jax.ShapeDtypeStruct(tuple(dims), kind)


def shards(
    inputs, w_query, w_key, w_value, bias_query, bias_value, w_out, bias_out, gain_one,
    shift_one, gain_two, shift_two, w_up, bias_up, w_down, bias_down, cotangent,
):
    count, tensors = lax.axis_size("shard"), lax.axis_size("tensor")
    tensor = lax.axis_index("tensor")
    frames_here, width = inputs.shape
    length = frames_here * tensors
    cols = w_query.shape[1]
    heads = cols // HD
    units = w_up.shape[1]
    scale = 1.0 / math.sqrt(HD)
    rows = w_query.shape[0]
    padded = -(-rows // 16) * 16
    row = lambda vector: vector.reshape(1, -1)
    pad = lambda block: jnp.pad(block, ((0, padded - rows), (0, 0)))
    join = lambda blocks: blocks[:, :rows].reshape(count * rows, blocks.shape[2])
    split = lambda whole: jnp.pad(
        whole.reshape(count, rows, whole.shape[1]), ((0, 0), (0, padded - rows), (0, 0))
    )
    w_attend = jnp.concatenate([w_query, w_key, w_value, w_out.T], axis=1)
    wide = w_attend.shape[1]
    block = (tensors, frames_here, width)
    vectors = jnp.concatenate(
        [gain_one, shift_one, bias_out, gain_two, shift_two, bias_down, gain_one, gain_one]
    ).reshape(8, width)
    bias_qkv = jnp.concatenate([
        lax.dynamic_slice_in_dim(bias_query, tensor * cols, cols),
        jnp.zeros((cols,), F32),
        lax.dynamic_slice_in_dim(bias_value, tensor * cols, cols),
    ])
    up_bias = lax.dynamic_slice_in_dim(bias_up, tensor * units, units)
    landing = [pltpu.VMEM((3, frames_here, width), BF16), pltpu.VMEM((frames_here, width), BF16)]

    n_copies = 5 * 4 + 3 * count
    (rows_one, cots, full_up, full_down, full_qkv, full_out, qkv, attended, hidden_state,
     rows_two) = call(
        functools.partial(front_kernel, count, heads, rows, scale),
        [VM] * 7,
        [shape(block), shape(block), shape((count, padded, units)),
         shape((count, padded, units)), shape((width, 3 * cols)), shape((width, cols)),
         shape((length, 3 * cols)), shape((length, cols)), shape((frames_here, width), F32),
         shape(block)],
        [pltpu.VMEM((count, padded, wide), BF16), pltpu.VMEM(block, BF16)] + landing
        + dma(n_copies) + [pltpu.SemaphoreType.DMA((4,))],
        (inputs, vectors, row(bias_qkv), cotangent, pad(w_attend), pad(w_up), pad(w_down.T)),
        "front", 0,
    )
    cots = cots.reshape(length, width)
    rows_two = rows_two.reshape(length, width)
    full_up, full_down = join(full_up), join(full_down)
    pre_act = jnp.dot(rows_two, full_up, preferred_element_type=F32) + up_bias
    activated = exact_gelu(pre_act).astype(BF16)
    grad_act = jnp.dot(cots, full_down, preferred_element_type=F32)
    grad_pre = jax.vjp(exact_gelu, pre_act)[1](grad_act)[0]
    grad_up_bias = jnp.sum(grad_pre, axis=0)
    grad_pre_low = grad_pre.astype(BF16)
    back_two = jnp.einsum("tf,df->td", grad_pre_low, full_up, preferred_element_type=F32)
    partial_two = jnp.einsum("tf,df->td", activated, full_down, preferred_element_type=F32)
    grad_down = jnp.einsum("td,tf->df", cots, activated, preferred_element_type=F32)
    grad_up = jnp.einsum("td,tf->df", rows_two, grad_pre_low, preferred_element_type=F32)
    half = count // 2
    n_copies = 5 * 4 + 3 * (2 * half - 1) + half + 3
    output, grad_inputs, sum_attend, sum_up, sum_down, totals = call(
        functools.partial(back_kernel, count, heads, rows, scale), [VM] * 14,
        [shape((frames_here, width), F32), shape((frames_here, width), F32),
         shape((padded, wide), F32), shape((padded, units), F32), shape((padded, units), F32),
         shape((tensors, 8, width), F32)],
        landing * 3
        + [pltpu.VMEM((half, padded, size), BF16) for size in (wide, units, units) * 2]
        + [pltpu.VMEM((frames_here, width), F32), pltpu.VMEM(block, BF16),
           pltpu.VMEM((length, cols), BF16), pltpu.VMEM((length, cols), F32),
           pltpu.VMEM((heads, HD, length), F32), pltpu.VMEM((heads, HD, length), F32),
           pltpu.VMEM((length, 3 * cols), BF16), pltpu.VMEM(block, BF16),
           pltpu.VMEM((width, 3 * cols), F32), pltpu.VMEM((width, cols), F32),
           pltpu.VMEM((count, padded, wide), BF16),
           pltpu.VMEM((8, width), F32), pltpu.VMEM((8, width), F32),
           pltpu.VMEM((half, 8, width), F32), pltpu.VMEM((tensors, 8, width), F32)]
        + dma(n_copies),
        (back_two.astype(BF16).reshape(block), partial_two.astype(BF16).reshape(block),
         hidden_state, cotangent, inputs, vectors, qkv, attended, rows_one, full_qkv, full_out,
         row(grad_up_bias), split(grad_up.astype(BF16)), split(grad_down.astype(BF16))),
        "back", 1,
    )
    (output, grad_inputs, grad_query, grad_key, grad_value, grad_w_out, grad_w_up, grad_w_down,
     sums) = call(
        functools.partial(finish_kernel, cols, rows), [VM] * 6,
        [shape((frames_here, width), F32), shape((frames_here, width), F32)]
        + [shape((rows, cols), F32)] * 3
        + [shape((cols, rows), F32), shape((rows, units), F32), shape((units, rows), F32),
           shape((8, width), F32)],
        [], (output, grad_inputs, sum_attend, sum_up, sum_down, totals), "finish",
    )
    return (
        output,
        grad_inputs,
        grad_query,
        grad_key,
        grad_value,
        totals[:, 4, :cols].reshape(-1),
        totals[:, 4, cols:2 * cols].reshape(-1),
        grad_w_out,
        sums[2],
        sums[6],
        sums[7],
        sums[0],
        sums[1],
        grad_w_up,
        totals[:, 5, :units].reshape(-1),
        grad_w_down,
        sums[3],
    )


def solution(mesh):
    placed = (
        P(("shard", "tensor"), None),
        P("shard", "tensor"),
        P("shard", "tensor"),
        P("shard", "tensor"),
        P(),
        P(),
        P("tensor", "shard"),
        P(),
        P(),
        P(),
        P(),
        P(),
        P("shard", "tensor"),
        P(),
        P("tensor", "shard"),
        P(),
        P(("shard", "tensor"), None),
    )
    return jax.shard_map(
        shards,
        mesh=mesh,
        in_specs=placed,
        out_specs=(
            P(("shard", "tensor"), None),
            P(("shard", "tensor"), None),
            P("shard", "tensor"),
            P("shard", "tensor"),
            P("shard", "tensor"),
            P(),
            P(),
            P("tensor", "shard"),
            P(),
            P(),
            P(),
            P(),
            P(),
            P("shard", "tensor"),
            P(),
            P("tensor", "shard"),
            P(),
        ),
        check_vma=False,
    )
```

time: 271 us -> 198 us (0.73)
  Pallas kernels: 200 us -> 155 us
  matrix products: 38.3 us -> 21.9 us
  local copies, waits for them, and re-layouts: 27.4 us -> 17.8 us
    pallas_call x6 -> x3, Pallas kernels: 200 us -> 155 us  [call(): pl.pallas_call(kernel, out_shape=list(outs), in_specs=ins, out_specs=[VM]...]
    dot_general x6 -> x0, matrix products: 16.8 us -> none  [the longest x1 4.25 us: shards(): jnp.dot(rows_one, full_qkv, preferred_element_type=F32) + bias_qkv]
    reshape x6 -> x2, local copies, waits for them, and re-layouts: 7.6 us -> 1.16 us  [shards(): row = lambda vector: vector.reshape(1, -1)]
    scatter x2 -> x0, local copies, waits for them, and re-layouts: 2.73 us -> none  [shards(): small.at[4, :2 * cols].set(bias_sums[0]).at[5, :units].set(grad_up_bias)]
    unnamed x28 -> x17, local copies, waits for them, and re-layouts: 6.04 us -> 7.62 us
where the time goes in v2:
time: 198 us; the launch traced here: 197 us
  Pallas kernels  155 us (78%)
  matrix products  21.9 us (11%)
  local copies, waits for them, and re-layouts  17.8 us (9%)
  other arithmetic  2.13 us (1%)
    pallas_call x3, Pallas kernels, call(): pl.pallas_call(kernel, out_shape=list(outs), in_specs=ins, out_specs=[VM]...  155 us
    dot_general x1, matrix products, shards(): grad_act = jnp.dot(cots, full_down, preferred_element_type=F32)  8.3 us
    unnamed x17, local copies, waits for them, and re-layouts  7.62 us

profile of v2, /device:TPU:0, one launch (start us, length us, event | category | flops | bytes accessed | tf_op | source)
XLA Modules:
  0.0 197.3 jit_solution(4910950692923529686)
XLA Ops:
  0.7 0.8 dynamic_slice.9
  1.4 0.8 dynamic_slice.10
  2.8 0.8 dynamic_slice.11
  4.3 0.7 constant_dynamic-update-slice_fusion.6
  5.0 0.7 constant_dynamic-update-slice_fusion.5
  5.7 0.7 constant_dynamic-update-slice_fusion.4
  7.1 0.7 constant_dynamic-update-slice_fusion.2
  7.8 0.7 constant_dynamic-update-slice_fusion.1
  8.5 0.7 constant_dynamic-update-slice_fusion
  9.8 0.9 copy.34
  10.7 1.6 pad_maximum_fusion.w0
  12.3 66.4 %front.1 = (bf16[4,256,768]{2,1,0:T(8,128)(2,1)}, bf16[4,256,768]{2,1,0:T(8,128)(2,1)}, bf16[8,96,768]{2,1,0:T(8,128)(2,1)}, bf16[8,96,768]{2,1,0:T(8,128)(2,1)}...) custom-call(bf16[256,768]{1,0:T(8,128)(2,1)} %x_ref.3, ...), custom_call_target="tpu_custom_call" | custom-call | tf_op jit(solution)/shard_map/front/pallas_call | solution.py:477
  78.7 3.3 %fusion.10 = f32[1024,768]{1,0:T(8,128)S(1)} fusion(bf16[1024,768]{1,0:T(8,128)(2,1)} %bitcast.32, bf16[768,768]{1,0:T(8,128)(2,1)} %bitcast.34), kind=kOutput, calls=%fused_computation.42 | convolution fusion | flops 1207959552 | bytes 5898240 | tf_op jit(solution)/shard_map/dot_general | solution.py:550
  82.0 8.3 %fusion.8 = (f32[768]{0:T(1024)S(1)}, bf16[1024,768]{1,0:T(8,128)(2,1)S(1)}, f32[1024,768]{1,0:T(8,128)S(1)}) fusion(f32[1024,768]{1,0:T(8,128)S(1)} %fusion.10, f32[768]{0:T(1024)S(1)} %dynamic_slice.11, bf16[1024,768]{1,0:T(8,128)(2,1)S(1)} %bitcast.30, bf16[768,768]{1,0:T(8,128)(2,1)S(1)} %bitcast.36), kind=kOutput, calls=%fused_computation.41 | convolution fusion | flops 1266154752 | bytes 10622976 | tf_op jit(solution)/shard_map/dot_general | solution.py:552
  90.4 2.5 %convolution_convert_fusion.3 = bf16[768,768]{1,0:T(8,128)(2,1)} fusion(bf16[1024,768]{1,0:T(8,128)(2,1)S(1)} %bitcast.33, bf16[1024,768]{1,0:T(8,128)(2,1)S(1)} %get-tuple-element.93), kind=kOutput, calls=%fused_computation.20 | convolution fusion | flops 1208549376 | bytes 4325376 | tf_op jit(solution)/shard_map/td,tf->df/dot_general | solution.py:559
  93.3 2.6 %convolution_convert_fusion.2 = bf16[768,768]{1,0:T(8,128)(2,1)} fusion(bf16[1024,768]{1,0:T(8,128)(2,1)S(1)} %bitcast.31, bf16[1024,768]{1,0:T(8,128)(2,1)S(1)} %multiply_convert_fusion), kind=kOutput, calls=%fused_computation.19 | convolution fusion | flops 1208549376 | bytes 4325376 | tf_op jit(solution)/shard_map/td,tf->df/dot_general | solution.py:558
  95.8 2.6 %convolution_convert_fusion = bf16[1024,768]{1,0:T(8,128)(2,1)} fusion(bf16[1024,768]{1,0:T(8,128)(2,1)S(1)} %multiply_convert_fusion, bf16[768,768]{1,0:T(8,128)(2,1)S(1)} %bitcast.37), kind=kOutput, calls=%fused_computation.17 | convolution fusion | flops 1208745984 | bytes 4325376 | tf_op jit(solution)/shard_map/tf,df->td/dot_general | solution.py:557
  99.0 2.7 %convolution_convert_fusion.1 = bf16[1024,768]{1,0:T(8,128)(2,1)} fusion(bf16[768,768]{1,0:T(8,128)(2,1)S(1)} %bitcast.35, bf16[1024,768]{1,0:T(8,128)(2,1)S(1)} %get-tuple-element.93), kind=kOutput, calls=%fused_computation.18 | convolution fusion | flops 1208745984 | bytes 4325376 | tf_op jit(solution)/shard_map/tf,df->td/dot_general | solution.py:556
  101.7 85.1 %back.1 = (f32[256,768]{1,0:T(8,128)}, f32[256,768]{1,0:T(8,128)}, f32[96,768]{1,0:T(8,128)}, f32[96,768]{1,0:T(8,128)}, f32[96,768]{1,0:T(8,128)}, /*index=5*/f32[4,8,768]{2,1,0:T(8,128)}) custom-call(bf16[4,256,768]{2,1,0:T(8,128)(2,1)} %bitcast.24, bf16[4,256,768]{2,1,0:T(8,128)(2,1)} %bitcast.23, f32[256,768]{1,0:T(8,128)} %get-tuple-element.46.hidden_ref, ...), custom_call_target="tpu_custom_call" | custom-call | tf_op jit(solution)/shard_map/back/pallas_call | solution.py:477
  186.8 0.9 slice_reduce_fusion
  189.0 1.5 slice.34
  190.5 3.3 %finish.1 = (f32[256,768]{1,0:T(8,128)}, f32[256,768]{1,0:T(8,128)}, f32[96,192]{1,0:T(8,128)}, f32[96,192]{1,0:T(8,128)}, f32[96,192]{1,0:T(8,128)}, /*index=5*...) custom-call(f32[256,768]{1,0:T(8,128)} %get-tuple-element.52.output_in, ...), custom_call_target="tpu_custom_call" | custom-call | tf_op jit(solution)/shard_map/finish/pallas_call | solution.py:477
  193.9 1.6 slice_reduce_fusion.2
  195.5 1.9 copy.35
  (19 shorter events, 5.0 us)
Async XLA Ops:
  78.7 3.3 %copy-start = (bf16[4,256,768]{2,1,0:T(8,128)(2,1)S(1)}, bf16[4,256,768]{2,1,0:T(8,128)(2,1)}, u32[]{:S(2)}) copy-start(bf16[4,256,768]{2,1,0:T(8,128)(2,1)} %get-tuple-element.44) | copy-start | bytes 4718596
  78.7 3.3 %copy-start.3 = (bf16[8,96,768]{2,1,0:T(8,128)(2,1)S(1)}, bf16[8,96,768]{2,1,0:T(8,128)(2,1)}, u32[]{:S(2)}) copy-start(bf16[8,96,768]{2,1,0:T(8,128)(2,1)} %get-tuple-element.45) | copy-start | bytes 3538948
  82.0 8.3 %copy-start.1 = (bf16[4,256,768]{2,1,0:T(8,128)(2,1)S(1)}, bf16[4,256,768]{2,1,0:T(8,128)(2,1)}, u32[]{:S(2)}) copy-start(bf16[4,256,768]{2,1,0:T(8,128)(2,1)} %get-tuple-element.42) | copy-start | bytes 4718596
  95.8 3.2 %copy-start.2 = (bf16[8,96,768]{2,1,0:T(8,128)(2,1)S(1)}, bf16[8,96,768]{2,1,0:T(8,128)(2,1)}, u32[]{:S(2)}) copy-start(bf16[8,96,768]{2,1,0:T(8,128)(2,1)} %get-tuple-element.43) | copy-start | bytes 3538948

commit v3 on v2

--- a/solution.py
+++ b/solution.py
@@ -155,9 +155,10 @@
     return ref[rows, begin:begin + HD]
 
 
-def front_kernel(count, heads, kept, scale, x_ref, vec_ref, bias_ref, cot_ref, w0, w1, w2,
-                 rows_ref, cots_ref, up_ref, down_ref, qkv_w, out_w, qkv_ref, attended_ref,
-                 hidden_ref, two_ref, attend_full, parts, landed, mixed, send, recv, local):
+def front_kernel(count, heads, kept, scale, x_ref, gain_a, shift_a, bias_o, gain_b, shift_b,
+                 bias_q, bias_v, bias_u, cot_ref, w0, w1, w2, up_row, rows_ref, cots_ref, up_ref, down_ref, qkv_w, out_w, qkv_ref, attended_ref,
+                 hidden_ref, two_ref, attend_full, parts, landed, mixed, vec_ref, bias_ref,
+                 send, recv, local):
     tensor, shard = lax.axis_index("tensor"), lax.axis_index("shard")
     partner = flip(shard, 1)
     peers = shard_peers_of(shard, count)
@@ -185,18 +186,35 @@
             passed[place].append(tally.copy(full.at[origin], full.at[origin], shard=partner))
 
     send_own(0)
+    for place, vector in enumerate((gain_a, shift_a, bias_o, gain_b, shift_b)):
+        vec_ref[place:place + 1, :] = vector[...].reshape(1, -1)
+    blocks = rows_ref.shape[0]
+
+    def own_part(vector):
+        whole = vector[...].reshape(1, -1)
+        size = whole.shape[1] // blocks
+        part = whole[:, :size]
+        for place in range(1, blocks):
+            part = jnp.where(tensor == place, whole[:, place * size:(place + 1) * size], part)
+        return part
+
+    query_part, value_part = own_part(bias_q), own_part(bias_v)
+    bias_ref[...] = jnp.concatenate(
+        [query_part, jnp.zeros_like(query_part), value_part], axis=1
+    )
+    up_row[...] = own_part(bias_u)
     gain_one, shift_one = vec_ref[0:1, :], vec_ref[1:2, :]
     rows_ref[tensor] = normalize(x_ref[...].astype(F32), gain_one, shift_one)[0].astype(BF16)
     rows_state = tensor_gather_start(tally, rows_ref, tensor)
     for keep in keeps:
         keep.start()
-    send_own(1)
-    send_own(2)
     for keep in keeps:
         keep.wait()
     tensor_gather_end(tally, rows_ref, tensor, rows_state)
+    forward(0)
+    send_own(1)
+    send_own(2)
     cot_state = tensor_gather_start(tally, cots_ref, tensor)
-    forward(0)
     for arrived in beside[:1] + passed[0]:
         arrived.wait_recv()
     width = heads * HD
@@ -300,7 +318,7 @@
 
 
 def back_kernel(count, heads, kept, scale, back_ref, two_ref, hidden_ref, cot_ref, x_ref,
-                vec_ref, qkv_ref, attended_ref, rows_ref, qkv_w, out_w, up_bias, g1, g2,
+                gain_a, gain_b, bias_d, qkv_ref, attended_ref, rows_ref, qkv_w, out_w, up_bias, g1, g2,
                 output_ref, inputs_ref, o0, o1, o2, total_ref,
                 landed0, mixed0, landed2, mixed2, landed1, mixed1, y0, y1, y2, z0, z1, z2,
                 grad_ref, rows_hidden, grad_att, dq, dk, dv, low, one_ref, acc_qkv, acc_out, g0,
@@ -320,7 +338,7 @@
     feed, feed_y, feed_z = (g1, g2), (y1, y2), (z1, z2)
     feed_sent = shard_sum_start(tally, feed, feed_y, shard, count)
     across = tensor_sum_pass(tally, back_ref, landed0, mixed0, tensor, state)
-    gain_one, gain_two = vec_ref[0:1, :], vec_ref[3:4, :]
+    gain_one, gain_two = gain_a[...].reshape(1, -1), gain_b[...].reshape(1, -1)
     _, unit, inverse = normalize(hidden_ref[...], gain_two, gain_two)
     normed = tensor_sum_end(back_ref, landed0, tensor, state, across)
     grad_rows, grad_gain, grad_shift = norm_backward(normed, unit, inverse, gain_two)
@@ -433,7 +451,7 @@
         for step in range(1, half)
     ]
     branch = tensor_sum_end(two_ref, landed2, tensor, two_state, two_across)
-    output_ref[...] = hidden_ref[...] + branch + vec_ref[5:6, :]
+    output_ref[...] = hidden_ref[...] + branch + bias_d[...].reshape(1, -1)
     shard_sum_end(feed, feed_y, feed_z, (o1, o2), shard, count, feed_across)
     for hop in hops:
         hop.wait_recv()
@@ -456,7 +474,8 @@
 
 def finish_kernel(cols, kept, output_in, inputs_in, attend_in, up_in, down_in, total_in,
                   output_ref, inputs_ref, query_ref, key_ref, value_ref, out_ref, up_ref,
-                  down_ref, sum_ref):
+                  down_ref, query_b, value_b, bias_o, gain_a, shift_a, gain_b, shift_b, bias_u,
+                  bias_d):
     output_ref[...] = output_in[...]
     inputs_ref[...] = inputs_in[...]
     query_ref[...] = attend_in[:kept, :cols]
@@ -464,8 +483,19 @@
     value_ref[...] = attend_in[:kept, 2 * cols:3 * cols]
     out_ref[...] = attend_in[:kept, 3 * cols:].T
     up_ref[...] = up_in[:kept, :]
-    down_ref[...] = down_in[:kept, :].T
-    sum_ref[...] = jnp.sum(total_in[...], axis=0)
+    down_ref[...] = down_in[:kept, :]
+    sums = jnp.sum(total_in[...], axis=0)
+    for ref, place in ((gain_b, 0), (shift_b, 1), (bias_o, 2), (bias_d, 3), (gain_a, 6),
+                       (shift_a, 7)):
+        ref[...] = sums[place:place + 1, :].reshape(-1)
+    tensors = total_in.shape[0]
+    units = up_in.shape[1]
+    for ref, place, begin, size in ((query_b, 4, 0, cols), (value_b, 4, cols, cols),
+                                    (bias_u, 5, 0, units)):
+        ref[...] = jnp.concatenate(
+            [total_in[spot, place:place + 1, begin:begin + size] for spot in range(tensors)],
+            axis=1,
+        ).reshape(-1)
 
 
 VM = pl.BlockSpec(memory_space=pltpu.VMEM)
@@ -519,29 +549,22 @@
     w_attend = jnp.concatenate([w_query, w_key, w_value, w_out.T], axis=1)
     wide = w_attend.shape[1]
     block = (tensors, frames_here, width)
-    vectors = jnp.concatenate(
-        [gain_one, shift_one, bias_out, gain_two, shift_two, bias_down, gain_one, gain_one]
-    ).reshape(8, width)
-    bias_qkv = jnp.concatenate([
-        lax.dynamic_slice_in_dim(bias_query, tensor * cols, cols),
-        jnp.zeros((cols,), F32),
-        lax.dynamic_slice_in_dim(bias_value, tensor * cols, cols),
-    ])
-    up_bias = lax.dynamic_slice_in_dim(bias_up, tensor * units, units)
     landing = [pltpu.VMEM((3, frames_here, width), BF16), pltpu.VMEM((frames_here, width), BF16)]
 
     n_copies = 5 * 4 + 3 * count
-    (rows_one, cots, full_up, full_down, full_qkv, full_out, qkv, attended, hidden_state,
+    (up_bias, rows_one, cots, full_up, full_down, full_qkv, full_out, qkv, attended, hidden_state,
      rows_two) = call(
         functools.partial(front_kernel, count, heads, rows, scale),
-        [VM] * 7,
-        [shape(block), shape(block), shape((count, padded, units)),
+        [VM] * 13,
+        [shape((1, units), F32), shape(block), shape(block), shape((count, padded, units)),
          shape((count, padded, units)), shape((width, 3 * cols)), shape((width, cols)),
          shape((length, 3 * cols)), shape((length, cols)), shape((frames_here, width), F32),
          shape(block)],
         [pltpu.VMEM((count, padded, wide), BF16), pltpu.VMEM(block, BF16)] + landing
+        + [pltpu.VMEM((8, width), F32), pltpu.VMEM((1, 3 * cols), F32)]
         + dma(n_copies) + [pltpu.SemaphoreType.DMA((4,))],
-        (inputs, vectors, row(bias_qkv), cotangent, pad(w_attend), pad(w_up), pad(w_down.T)),
+        (inputs, gain_one, shift_one, bias_out, gain_two, shift_two, bias_query, bias_value,
+         bias_up, cotangent, pad(w_attend), pad(w_up), pad(w_down.T)),
         "front", 0,
     )
     cots = cots.reshape(length, width)
@@ -560,7 +583,7 @@
     half = count // 2
     n_copies = 5 * 4 + 3 * (2 * half - 1) + half + 3
     output, grad_inputs, sum_attend, sum_up, sum_down, totals = call(
-        functools.partial(back_kernel, count, heads, rows, scale), [VM] * 14,
+        functools.partial(back_kernel, count, heads, rows, scale), [VM] * 16,
         [shape((frames_here, width), F32), shape((frames_here, width), F32),
          shape((padded, wide), F32), shape((padded, units), F32), shape((padded, units), F32),
          shape((tensors, 8, width), F32)],
@@ -576,37 +599,39 @@
            pltpu.VMEM((half, 8, width), F32), pltpu.VMEM((tensors, 8, width), F32)]
         + dma(n_copies),
         (back_two.astype(BF16).reshape(block), partial_two.astype(BF16).reshape(block),
-         hidden_state, cotangent, inputs, vectors, qkv, attended, rows_one, full_qkv, full_out,
+         hidden_state, cotangent, inputs, gain_one, gain_two, bias_down, qkv, attended, rows_one, full_qkv, full_out,
          row(grad_up_bias), split(grad_up.astype(BF16)), split(grad_down.astype(BF16))),
         "back", 1,
     )
     (output, grad_inputs, grad_query, grad_key, grad_value, grad_w_out, grad_w_up, grad_w_down,
-     sums) = call(
+     *sums) = call(
         functools.partial(finish_kernel, cols, rows), [VM] * 6,
         [shape((frames_here, width), F32), shape((frames_here, width), F32)]
         + [shape((rows, cols), F32)] * 3
-        + [shape((cols, rows), F32), shape((rows, units), F32), shape((units, rows), F32),
-           shape((8, width), F32)],
+        + [shape((cols, rows), F32), shape((rows, units), F32), shape((rows, units), F32)]
+        + [shape((width,), F32)] * 7 + [shape(bias_up.shape, F32), shape((width,), F32)],
         [], (output, grad_inputs, sum_attend, sum_up, sum_down, totals), "finish",
     )
+    (grad_query_bias, grad_value_bias, grad_bias_out, grad_gain_one, grad_shift_one,
+     grad_gain_two, grad_shift_two, grad_bias_up, grad_bias_down) = sums
     return (
         output,
         grad_inputs,
         grad_query,
         grad_key,
         grad_value,
-        totals[:, 4, :cols].reshape(-1),
-        totals[:, 4, cols:2 * cols].reshape(-1),
+        grad_query_bias,
+        grad_value_bias,
         grad_w_out,
-        sums[2],
-        sums[6],
-        sums[7],
-        sums[0],
-        sums[1],
+        grad_bias_out,
+        grad_gain_one,
+        grad_shift_one,
+        grad_gain_two,
+        grad_shift_two,
         grad_w_up,
-        totals[:, 5, :units].reshape(-1),
-        grad_w_down,
-        sums[3],
+        grad_bias_up,
+        grad_w_down.T,
+        grad_bias_down,
     )
 
 

time: 198 us -> 181 us (0.914)
  local copies, waits for them, and re-layouts: 17.8 us -> 1.48 us
    unnamed x17 -> x9, local copies, waits for them, and re-layouts: 7.62 us -> 0.9 us
    slice x3 -> x0, local copies, waits for them, and re-layouts: 4.05 us -> none  [the longest x1 1.62 us: shards(): sums[3]]
    dynamic_slice x3 -> x0, local copies, waits for them, and re-layouts: 2.29 us -> none  [the longest x1 0.77 us: shards(): up_bias = lax.dynamic_slice_in_dim(bias_up, tensor * units, units)]
where the time goes in v3:
time: 181 us
  Pallas kernels  154 us (85%)
  matrix products  21.7 us (12%)
  other arithmetic  2.73 us (2%)
    pallas_call x3, Pallas kernels, call(): pl.pallas_call(kernel, out_shape=list(outs), in_specs=ins, out_specs=[VM]...  154 us
    dot_general x1, matrix products, shards(): grad_act = jnp.dot(cots, full_down, preferred_element_type=F32)  8.3 us

profile of v3, /device:TPU:0, one launch (start us, length us, event | category | flops | bytes accessed | tf_op | source)
XLA Modules:
  0.0 181.0 jit_solution(4279729868507912016)
XLA Ops:
  0.7 0.9 copy.34
  1.5 1.6 pad_maximum_fusion.w0
  3.2 66.6 %front.1 = (f32[1,768]{1,0:T(1,128)}, bf16[4,256,768]{2,1,0:T(8,128)(2,1)}, bf16[4,256,768]{2,1,0:T(8,128)(2,1)}, bf16[8,96,768]{2,1,0:T(8,128)(2,1)}, bf16[8,96...) custom-call(bf16[256,768]{1,0:T(8,128)(2,1)} %x_ref.3, ...), custom_call_target="tpu_custom_call" | custom-call | tf_op jit(solution)/shard_map/front/pallas_call | solution.py:507
  69.8 0.7 reduce
  70.5 0.0 copy-start
  70.5 0.0 copy-start.3
  70.5 3.3 %fusion.10 = f32[1024,768]{1,0:T(8,128)S(1)} fusion(bf16[1024,768]{1,0:T(8,128)(2,1)} %bitcast.31, bf16[768,768]{1,0:T(8,128)(2,1)} %bitcast.33), kind=kOutput, calls=%fused_computation.25 | convolution fusion | flops 1207959552 | bytes 5898240 | tf_op jit(solution)/shard_map/dot_general | solution.py:573
  73.8 0.0 copy-done
  73.8 0.0 copy-done.3
  73.8 0.0 copy-start.1
  73.8 8.3 %fusion.8 = (f32[768]{0:T(1024)S(1)}, bf16[1024,768]{1,0:T(8,128)(2,1)S(1)}, f32[1024,768]{1,0:T(8,128)S(1)}) fusion(f32[1024,768]{1,0:T(8,128)S(1)} %fusion.10, f32[768]{0:T(1024)S(1)} %reduce, bf16[1024,768]{1,0:T(8,128)(2,1)S(1)} %bitcast.29, bf16[768,768]{1,0:T(8,128)(2,1)S(1)} %bitcast.35), kind=kOutput, calls=%fused_computation.24 | convolution fusion | flops 1266154752 | bytes 10622976 | tf_op jit(solution)/shard_map/dot_general | solution.py:575
  82.1 0.0 copy-done.1
  82.1 2.5 %convolution_convert_fusion.3 = bf16[768,768]{1,0:T(8,128)(2,1)} fusion(bf16[1024,768]{1,0:T(8,128)(2,1)S(1)} %bitcast.32, bf16[1024,768]{1,0:T(8,128)(2,1)S(1)} %get-tuple-element.86), kind=kOutput, calls=%fused_computation.20 | convolution fusion | flops 1208549376 | bytes 4325376 | tf_op jit(solution)/shard_map/td,tf->df/dot_general | solution.py:582
  84.6 0.4 multiply_convert_fusion
  85.1 2.5 %convolution_convert_fusion.2 = bf16[768,768]{1,0:T(8,128)(2,1)} fusion(bf16[1024,768]{1,0:T(8,128)(2,1)S(1)} %bitcast.30, bf16[1024,768]{1,0:T(8,128)(2,1)S(1)} %multiply_convert_fusion), kind=kOutput, calls=%fused_computation.19 | convolution fusion | flops 1208549376 | bytes 4325376 | tf_op jit(solution)/shard_map/td,tf->df/dot_general | solution.py:581
  87.6 0.0 copy-start.2
  87.6 2.6 %convolution_convert_fusion = bf16[1024,768]{1,0:T(8,128)(2,1)} fusion(bf16[1024,768]{1,0:T(8,128)(2,1)S(1)} %multiply_convert_fusion, bf16[768,768]{1,0:T(8,128)(2,1)S(1)} %bitcast.36), kind=kOutput, calls=%fused_computation.17 | convolution fusion | flops 1208745984 | bytes 4325376 | tf_op jit(solution)/shard_map/tf,df->td/dot_general | solution.py:580
  90.1 0.6 reshape.67.up_bias
  90.7 0.0 copy-done.2
  90.7 2.6 %convolution_convert_fusion.1 = bf16[1024,768]{1,0:T(8,128)(2,1)} fusion(bf16[768,768]{1,0:T(8,128)(2,1)S(1)} %bitcast.34, bf16[1024,768]{1,0:T(8,128)(2,1)S(1)} %get-tuple-element.86), kind=kOutput, calls=%fused_computation.18 | convolution fusion | flops 1208745984 | bytes 4325376 | tf_op jit(solution)/shard_map/tf,df->td/dot_general | solution.py:579
  93.3 84.3 %back.1 = (f32[256,768]{1,0:T(8,128)}, f32[256,768]{1,0:T(8,128)}, f32[96,768]{1,0:T(8,128)}, f32[96,768]{1,0:T(8,128)}, f32[96,768]{1,0:T(8,128)}, /*index=5*/f32[4,8,768]{2,1,0:T(8,128)}) custom-call(bf16[4,256,768]{2,1,0:T(8,128)(2,1)} %bitcast.24, bf16[4,256,768]{2,1,0:T(8,128)(2,1)} %bitcast.23, f32[256,768]{1,0:T(8,128)} %get-tuple-element.56.hidden_ref, ...), custom_call_target="tpu_custom_call" | custom-call | tf_op jit(solution)/shard_map/back/pallas_call | solution.py:507
  177.6 3.3 %finish.1 = (f32[256,768]{1,0:T(8,128)}, f32[256,768]{1,0:T(8,128)}, f32[96,192]{1,0:T(8,128)}, f32[96,192]{1,0:T(8,128)}, f32[96,192]{1,0:T(8,128)}, /*index=5*...) custom-call(f32[256,768]{1,0:T(8,128)} %get-tuple-element.62.output_, ...), custom_call_target="tpu_custom_call" | custom-call | tf_op jit(solution)/shard_map/finish/pallas_call | solution.py:507
Async XLA Ops:
  70.5 3.3 %copy-start = (bf16[4,256,768]{2,1,0:T(8,128)(2,1)S(1)}, bf16[4,256,768]{2,1,0:T(8,128)(2,1)}, u32[]{:S(2)}) copy-start(bf16[4,256,768]{2,1,0:T(8,128)(2,1)} %get-tuple-element.54) | copy-start | bytes 4718596
  70.5 3.3 %copy-start.3 = (bf16[8,96,768]{2,1,0:T(8,128)(2,1)S(1)}, bf16[8,96,768]{2,1,0:T(8,128)(2,1)}, u32[]{:S(2)}) copy-start(bf16[8,96,768]{2,1,0:T(8,128)(2,1)} %get-tuple-element.55) | copy-start | bytes 3538948
  73.8 8.3 %copy-start.1 = (bf16[4,256,768]{2,1,0:T(8,128)(2,1)S(1)}, bf16[4,256,768]{2,1,0:T(8,128)(2,1)}, u32[]{:S(2)}) copy-start(bf16[4,256,768]{2,1,0:T(8,128)(2,1)} %get-tuple-element.51) | copy-start | bytes 4718596
  87.6 3.2 %copy-start.2 = (bf16[8,96,768]{2,1,0:T(8,128)(2,1)S(1)}, bf16[8,96,768]{2,1,0:T(8,128)(2,1)}, u32[]{:S(2)}) copy-start(bf16[8,96,768]{2,1,0:T(8,128)(2,1)} %get-tuple-element.52) | copy-start | bytes 3538948
